TPU v7x, 32 devices: a whole 2x2x4 slice. The times are simulated.
32 devices in a mesh: rep: 4 (over y, x), seq: 4 (over z), grp: 2 (over core).
Axes of the slice: x: 2, y: 2, z: 4, core: 2. Of those that a mesh axis runs over, the one named last changes fastest.
Arguments:
- tokens: bfloat16 [8192, 768], P(('rep', 'seq', 'grp')), may hold values from -24 to 24
- cotangent: bfloat16 [8192, 768], P(('rep', 'seq', 'grp')), may hold values from -6 to 6
- item_lengths: int32 [4, 4], P('rep'), may hold values from 64 to 1792, as said below
- qkv_weight: float32 [768, 2304], P(('seq', 'grp')), may hold values from -0.3125 to 0.3125
- qkv_first: float32 [768, 2304], P(('seq', 'grp')), may hold values from -0.00061035156 to 0.00061035156
- qkv_second: float32 [768, 2304], P(('seq', 'grp')), may hold values from 7.064254e-11 to 1.1302806e-09
- out_weight: float32 [768, 768], P(('seq', 'grp')), may hold values from -0.21875 to 0.21875
- out_first: float32 [768, 768], P(('seq', 'grp')), may hold values from -0.00061035156 to 0.00061035156
- out_second: float32 [768, 768], P(('seq', 'grp')), may hold values from 7.064254e-11 to 1.1302806e-09
- up_weight: float32 [768, 3072], P(('seq', 'grp')), may hold values from -0.21875 to 0.21875
- up_first: float32 [768, 3072], P(('seq', 'grp')), may hold values from -0.00061035156 to 0.00061035156
- up_second: float32 [768, 3072], P(('seq', 'grp')), may hold values from 7.064254e-11 to 1.1302806e-09
- down_weight: float32 [3072, 768], P(('seq', 'grp')), may hold values from -0.109375 to 0.109375
- down_first: float32 [3072, 768], P(('seq', 'grp')), may hold values from -0.00061035156 to 0.00061035156
- down_second: float32 [3072, 768], P(('seq', 'grp')), may hold values from 7.064254e-11 to 1.1302806e-09
- norm_params: float32 [4, 768], P(None, ('seq', 'grp')), may hold values from -1.2 to 2.4, as said below
- norm_first: float32 [4, 768], P(None, ('seq', 'grp')), may hold values from -0.001953125 to 0.001953125
- norm_second: float32 [4, 768], P(None, ('seq', 'grp')), may hold values from 6.3578287e-10 to 1.0172526e-08
- conv_kernel: float32 [12, 33], replicated, may hold values from -1 to 1
- conv_first: float32 [12, 33], replicated, may hold values from -0.005859375 to 0.005859375
- conv_second: float32 [12, 33], replicated, may hold values from 7.064254e-09 to 1.13028065e-07
Outputs:
- output: bfloat16 [8192, 768], P(('rep', 'seq', 'grp'))
- input_grad: bfloat16 [8192, 768], P(('rep', 'seq', 'grp'))
- grad_norm: float32 [], replicated
- qkv_new: float32 [768, 2304], P(('seq', 'grp'))
- qkv_first_new: float32 [768, 2304], P(('seq', 'grp'))
- qkv_second_new: float32 [768, 2304], P(('seq', 'grp'))
- out_new: float32 [768, 768], P(('seq', 'grp'))
- out_first_new: float32 [768, 768], P(('seq', 'grp'))
- out_second_new: float32 [768, 768], P(('seq', 'grp'))
- up_new: float32 [768, 3072], P(('seq', 'grp'))
- up_first_new: float32 [768, 3072], P(('seq', 'grp'))
- up_second_new: float32 [768, 3072], P(('seq', 'grp'))
- down_new: float32 [3072, 768], P(('seq', 'grp'))
- down_first_new: float32 [3072, 768], P(('seq', 'grp'))
- down_second_new: float32 [3072, 768], P(('seq', 'grp'))
- norm_new: float32 [4, 768], P(None, ('seq', 'grp'))
- norm_first_new: float32 [4, 768], P(None, ('seq', 'grp'))
- norm_second_new: float32 [4, 768], P(None, ('seq', 'grp'))
- conv_new: float32 [12, 33], replicated
- conv_first_new: float32 [12, 33], replicated
- conv_second_new: float32 [12, 33], replicated
Inputs may be any that keep to these rules, and one draw needn't show every extreme that they name: `item_lengths`: items 0, 2 and 3 have 64 to 96 tokens: one of them exactly 96, the other two together 64 + 96; item 1 takes the rest of the group's 2048 tokens, 1792. `norm_params`: rows 0 and 2 are positive gains.
All inputs are finite; a program needn't handle non-finite values.
Results may differ from a plain program's by a relative error of at most 0.018.
Values may be sent and summed in bfloat16 or wider, within the bound.
A program may use at most 256 MiB of HBM per device.

v0:
```python
import jax
import jax.numpy as jnp
from jax import lax
from jax.sharding import PartitionSpec as P

D = 768
HEADS = 12
HEAD = 64
LAND = 64
KERNEL = 33
HALO = 16
NS_STEPS = 6
ITEMS = 4
STEP = 10
TOK_DEV = 256


HIGHEST_PREC = lax.Precision.HIGHEST
EPS_NORM = 1e-05
BETA_ONE = 0.9
BETA_TWO = 0.999
ADAM_EPS = 1e-08
RATE_MATRIX = 0.02
RATE_NORM = 0.3
RATE_CONV = 0.1
DECAY_RATE = 0.01
MAX_NORM = 1.0


def extended(cells, sides, width):
    for axis, dim in sides:
        count = lax.axis_size(axis)
        ends = count - 1
        head = lax.slice_in_dim(cells, 0, width, axis=dim)
        tail = lax.slice_in_dim(cells, cells.shape[dim] - width, cells.shape[dim], axis=dim)
        cells = jnp.concatenate(
            [
                lax.ppermute(tail, axis, [(i, (i + 1) % count) for i in range(ends)]),
                cells,
                lax.ppermute(head, axis, [((i + 1) % count, i) for i in range(ends)]),
            ],
            axis=dim,
        )
    return cells


def locate(positions, lengths):
    ends = jnp.cumsum(lengths)
    starts = ends - lengths
    inside = (positions[:, None] >= starts[None, :]) & (positions[:, None] < ends[None, :])
    item_ids = jnp.sum((positions[:, None] >= ends[None, :]).astype(jnp.int32), axis=1)
    valid = (positions >= 0) & (positions < ends[-1])
    item_ids = jnp.where(valid, item_ids, -1)
    own_len = jnp.sum(jnp.where(inside, lengths[None, :], 0), axis=1)
    own_start = jnp.sum(jnp.where(inside, starts[None, :], 0), axis=1)
    segment = (positions - own_start) * LAND // jnp.maximum(own_len, 1)
    columns = jnp.where(valid, item_ids * LAND + segment, -1)
    return (item_ids, columns)


def landmark_counts(lengths):
    marks = jnp.arange(LAND + 1, dtype=jnp.int32)
    edges = (marks[None, :] * lengths[:, None] + LAND - 1) // LAND
    return (edges[:, 1:] - edges[:, :-1]).reshape(-1)


def layer_norm(hidden, gain_row, shift_row):
    row_mean = jnp.mean(hidden, axis=-1, keepdims=True)
    centred = hidden - row_mean
    variance = jnp.mean(centred * centred, axis=-1, keepdims=True)
    return centred * lax.rsqrt(variance + EPS_NORM) * gain_row + shift_row


def gelu_exact(values):
    return jax.nn.gelu(values, approximate=False)


def mixing_rest(mark_scores, num_all, den_all):
    key_values = (
        num_all.reshape(ITEMS, LAND, HEADS, HEAD) / den_all.reshape(ITEMS, LAND, HEADS)[..., None]
    )
    kernel_two = jax.nn.softmax(mark_scores, axis=-1)
    frobenius = jnp.sum(kernel_two * kernel_two, axis=(2, 3), keepdims=True)
    inverse = jnp.swapaxes(kernel_two, 2, 3) / frobenius
    identity = jnp.eye(LAND, dtype=kernel_two.dtype)
    for iteration in range(NS_STEPS):
        product = jnp.einsum("ahjk,ahkl->ahjl", kernel_two, inverse, precision=HIGHEST_PREC)
        inner = 7.0 * identity - product
        inner = 15.0 * identity - jnp.einsum(
            "ahjk,ahkl->ahjl", product, inner, precision=HIGHEST_PREC
        )
        inner = 13.0 * identity - jnp.einsum(
            "ahjk,ahkl->ahjl", product, inner, precision=HIGHEST_PREC
        )
        inverse = 0.25 * jnp.einsum("ahjk,ahkl->ahjl", inverse, inner, precision=HIGHEST_PREC)
    mixed_rows = jnp.einsum("ahjk,akhd->ajhd", inverse, key_values, precision=HIGHEST_PREC)
    return mixed_rows.reshape(ITEMS * LAND, HEADS * HEAD)


def adamw(weight, moment_one, moment_two, gradient, clip_factor, rate_value, decay_value):
    clipped = gradient * clip_factor
    moment_one = BETA_ONE * moment_one + (1.0 - BETA_ONE) * clipped
    moment_two = BETA_TWO * moment_two + (1.0 - BETA_TWO) * clipped * clipped
    first_hat = moment_one / (1.0 - BETA_ONE**STEP)
    second_hat = moment_two / (1.0 - BETA_TWO**STEP)
    weight = weight - rate_value * (
        first_hat / (jnp.sqrt(second_hat) + ADAM_EPS) + decay_value * weight
    )
    return (weight, moment_one, moment_two)


def contract_rows(left, right):
    return lax.dot_general(
        left, right, (((0,), (0,)), ((), ())), preferred_element_type=jnp.float32
    )


def contract_cols(left, right):
    return lax.dot_general(
        left, right, (((1,), (1,)), ((), ())), preferred_element_type=jnp.float32
    )


def on_device(
    tokens,
    cotangent,
    item_lengths,
    qkv_weight,
    qkv_first,
    qkv_second,
    out_weight,
    out_first,
    out_second,
    up_weight,
    up_first,
    up_second,
    down_weight,
    down_first,
    down_second,
    norm_params,
    norm_first,
    norm_second,
    conv_kernel,
    conv_first,
    conv_second,
):
    temper = HEAD ** (-0.5)
    col_total = ITEMS * LAND
    w_qkv, w_out, w_up, w_down, gains_low = (
        lax.all_gather(qkv_weight.astype(jnp.bfloat16), ("seq", "grp"), axis=0, tiled=True),
        lax.all_gather(out_weight.astype(jnp.bfloat16), ("seq", "grp"), axis=0, tiled=True),
        lax.all_gather(up_weight.astype(jnp.bfloat16), ("seq", "grp"), axis=0, tiled=True),
        lax.all_gather(down_weight.astype(jnp.bfloat16), ("seq", "grp"), axis=0, tiled=True),
        lax.all_gather(norm_params.astype(jnp.bfloat16), ("seq", "grp"), axis=1, tiled=True),
    )
    gains_all = gains_low.astype(jnp.float32)
    lengths = item_lengths[0]
    first_row = lax.axis_index(("seq", "grp")) * TOK_DEV
    positions = first_row - HALO + jnp.arange(TOK_DEV + 2 * HALO, dtype=jnp.int32)
    item_ext, column_ext = locate(positions, lengths)
    item_mid = item_ext[HALO : HALO + TOK_DEV]
    column_mid = column_ext[HALO : HALO + TOK_DEV]
    col_ids = jnp.arange(col_total, dtype=jnp.int32)
    col_hot = (column_mid[:, None] == col_ids[None, :]).astype(jnp.bfloat16)
    member = (item_mid[:, None] == (col_ids // LAND)[None, :]).astype(jnp.float32)
    counts_f = landmark_counts(lengths).astype(jnp.float32)
    projected = jnp.dot(tokens, w_qkv, preferred_element_type=jnp.float32)
    proj_low = projected.astype(jnp.bfloat16)
    queries = proj_low[:, :D]
    key_rows = proj_low[:, D : 2 * D]
    value_rows = proj_low[:, 2 * D :]
    land_sums = lax.psum(contract_rows(col_hot, proj_low[:, : 2 * D]), ("seq", "grp"))
    mean_q = (land_sums[:, :D] / counts_f[:, None]).astype(jnp.bfloat16)
    mean_k = (land_sums[:, D:] / counts_f[:, None]).astype(jnp.bfloat16)
    query_heads = queries.reshape(TOK_DEV, HEADS, HEAD)
    key_heads = key_rows.reshape(TOK_DEV, HEADS, HEAD)
    value_heads = value_rows.reshape(TOK_DEV, HEADS, HEAD)
    mean_q3 = mean_q.reshape(col_total, HEADS, HEAD)
    mean_k3 = mean_k.reshape(col_total, HEADS, HEAD)
    scores_key = (
        jnp.einsum("chd,phd->chp", mean_q3, key_heads, preferred_element_type=jnp.float32) * temper
    )
    expo_key = jnp.exp(scores_key) * jnp.transpose(member)[:, None, :]
    expo_low = expo_key.astype(jnp.bfloat16)
    num_part = jnp.einsum(
        "chp,phd->chd", expo_low, value_heads, preferred_element_type=jnp.float32
    ).reshape(col_total, D)
    num_all, den_all = lax.psum((num_part, jnp.sum(expo_key, axis=2)), ("seq", "grp"))
    query_marks4 = mean_q.reshape(ITEMS, LAND, HEADS, HEAD)
    key_marks4 = mean_k.reshape(ITEMS, LAND, HEADS, HEAD)
    mark_scores = (
        jnp.einsum("ajhd,akhd->ahjk", query_marks4, key_marks4, preferred_element_type=jnp.float32)
        * temper
    )
    mixed_rows, mix_pull = jax.vjp(mixing_rest, mark_scores, num_all, den_all)
    mixed3 = mixed_rows.astype(jnp.bfloat16).reshape(col_total, HEADS, HEAD)
    scores_tok = (
        jnp.einsum("phd,chd->phc", query_heads, mean_k3, preferred_element_type=jnp.float32)
        * temper
    )
    expo_tok = jnp.exp(scores_tok) * member[:, None, :]
    attn_probs = expo_tok / jnp.sum(expo_tok, axis=2, keepdims=True)
    probs_low = attn_probs.astype(jnp.bfloat16)
    attended = jnp.einsum(
        "phc,chd->phd", probs_low, mixed3, preferred_element_type=jnp.float32
    ).reshape(TOK_DEV, D)
    value_ext = extended(value_rows, ((("seq", "grp"), 0),), HALO)
    channel_taps = jnp.repeat(conv_kernel, HEAD, axis=0)
    same_masks = [
        (item_ext[offset : offset + TOK_DEV] == item_mid).astype(jnp.float32)
        for offset in range(KERNEL)
    ]
    conv_out = jnp.zeros((TOK_DEV, D), jnp.float32)
    for offset in range(KERNEL):
        conv_out = conv_out + value_ext[offset : offset + TOK_DEV] * (
            channel_taps[:, offset][None, :] * same_masks[offset][:, None]
        )
    branch = (attended + conv_out).astype(jnp.bfloat16)
    attn_out = jnp.dot(branch, w_out, preferred_element_type=jnp.float32)
    normed_one, norm_one_pull = jax.vjp(
        layer_norm, tokens.astype(jnp.float32) + attn_out, gains_all[0], gains_all[1]
    )
    normed_low = normed_one.astype(jnp.bfloat16)
    up_out = jnp.dot(normed_low, w_up, preferred_element_type=jnp.float32)
    activated, gelu_pull = jax.vjp(gelu_exact, up_out)
    act_low = activated.astype(jnp.bfloat16)
    down_out = jnp.dot(act_low, w_down, preferred_element_type=jnp.float32)
    result, norm_two_pull = jax.vjp(layer_norm, normed_one + down_out, gains_all[2], gains_all[3])
    d_hidden_two, d_gain_two, d_shift_two = norm_two_pull(cotangent.astype(jnp.float32))
    d_down_low = d_hidden_two.astype(jnp.bfloat16)
    grad_down = contract_rows(act_low, d_down_low)
    (d_up,) = gelu_pull(contract_cols(d_down_low, w_down))
    d_up_low = d_up.astype(jnp.bfloat16)
    grad_up = contract_rows(normed_low, d_up_low)
    d_normed = d_hidden_two + contract_cols(d_up_low, w_up)
    d_hidden_one, d_gain_one, d_shift_one = norm_one_pull(d_normed)
    d_attn_low = d_hidden_one.astype(jnp.bfloat16)
    grad_out = contract_rows(branch, d_attn_low)
    d_branch_low = contract_cols(d_attn_low, w_out).astype(jnp.bfloat16)
    d_branch_f = d_branch_low.astype(jnp.float32)
    d_branch_ext = extended(d_branch_low, ((("seq", "grp"), 0),), HALO)
    d_values_conv = jnp.zeros((TOK_DEV, D), jnp.float32)
    tap_grads = []
    for offset in range(KERNEL):
        d_values_conv = d_values_conv + d_branch_ext[offset : offset + TOK_DEV] * (
            channel_taps[:, KERNEL - 1 - offset][None, :] * same_masks[offset][:, None]
        )
        tap_grads.append(
            jnp.sum(
                d_branch_f * value_ext[offset : offset + TOK_DEV] * same_masks[offset][:, None],
                axis=0,
            )
        )
    grad_conv = jnp.sum(jnp.stack(tap_grads, axis=1).reshape(HEADS, HEAD, KERNEL), axis=1)
    d_attended = d_branch_low.reshape(TOK_DEV, HEADS, HEAD)
    d_mixed_part = jnp.einsum(
        "phc,phd->chd", probs_low, d_attended, preferred_element_type=jnp.float32
    ).reshape(col_total, D)
    d_probs = jnp.einsum("phd,chd->phc", d_attended, mixed3, preferred_element_type=jnp.float32)
    d_scores_tok = (
        attn_probs * (d_probs - jnp.sum(attn_probs * d_probs, axis=2, keepdims=True))
    ).astype(jnp.bfloat16)
    d_query_tok = (
        jnp.einsum("phc,chd->phd", d_scores_tok, mean_k3, preferred_element_type=jnp.float32)
        * temper
    )
    d_meank_part = (
        jnp.einsum(
            "phc,phd->chd", d_scores_tok, query_heads, preferred_element_type=jnp.float32
        ).reshape(col_total, D)
        * temper
    )
    d_mixed, d_meank_tok = lax.psum((d_mixed_part, d_meank_part), ("seq", "grp"))
    d_mark_scores, d_num, d_den = mix_pull(d_mixed)
    d_mark_scaled = d_mark_scores * temper
    d_mean_q_mix = jnp.einsum(
        "ahjk,akhd->ajhd", d_mark_scaled, key_marks4.astype(jnp.float32), precision=HIGHEST_PREC
    ).reshape(col_total, D)
    d_mean_k_mix = jnp.einsum(
        "ahjk,ajhd->akhd", d_mark_scaled, query_marks4.astype(jnp.float32), precision=HIGHEST_PREC
    ).reshape(col_total, D)
    d_num3 = d_num.reshape(col_total, HEADS, HEAD)
    d_expo = d_den[:, :, None] + jnp.einsum(
        "chd,phd->chp", d_num3, value_heads.astype(jnp.float32), precision=HIGHEST_PREC
    )
    d_scores_key = (expo_key * d_expo).astype(jnp.bfloat16)
    d_key_mix = (
        jnp.einsum("chp,chd->phd", d_scores_key, mean_q3, preferred_element_type=jnp.float32)
        * temper
    )
    d_meanq_part = (
        jnp.einsum(
            "chp,phd->chd", d_scores_key, key_heads, preferred_element_type=jnp.float32
        ).reshape(col_total, D)
        * temper
    )
    d_value_mix = jnp.einsum(
        "chp,chd->phd", expo_low.astype(jnp.float32), d_num3, precision=HIGHEST_PREC
    )
    d_meanq_tok = lax.psum(d_meanq_part, ("seq", "grp"))
    d_sums = (
        jnp.concatenate([d_mean_q_mix + d_meanq_tok, d_mean_k_mix + d_meank_tok], axis=1)
        / counts_f[:, None]
    )
    d_land_rows = jnp.dot(col_hot.astype(jnp.float32), d_sums, precision=HIGHEST_PREC)
    d_queries = d_query_tok.reshape(TOK_DEV, D) + d_land_rows[:, :D]
    d_keys = d_key_mix.reshape(TOK_DEV, D) + d_land_rows[:, D:]
    d_values = d_value_mix.reshape(TOK_DEV, D) + d_values_conv
    d_proj_low = jnp.concatenate([d_queries, d_keys, d_values], axis=1).astype(jnp.bfloat16)
    grad_qkv = contract_rows(tokens, d_proj_low)
    input_grad = (d_hidden_one + contract_cols(d_proj_low, w_qkv)).astype(jnp.bfloat16)
    grad_norms = jnp.stack([d_gain_one, d_shift_one, d_gain_two, d_shift_two])
    group_qkv, group_out, group_up, group_down, group_norm = (
        lax.psum_scatter(grad_qkv, ("seq", "grp"), scatter_dimension=0, tiled=True),
        lax.psum_scatter(grad_out, ("seq", "grp"), scatter_dimension=0, tiled=True),
        lax.psum_scatter(grad_up, ("seq", "grp"), scatter_dimension=0, tiled=True),
        lax.psum_scatter(grad_down, ("seq", "grp"), scatter_dimension=0, tiled=True),
        lax.psum_scatter(grad_norms, ("seq", "grp"), scatter_dimension=1, tiled=True),
    )
    shard_qkv, shard_out, shard_up, shard_down, shard_norm, conv_rep = (
        lax.psum(group_qkv.astype(jnp.bfloat16), "rep").astype(jnp.float32),
        lax.psum(group_out.astype(jnp.bfloat16), "rep").astype(jnp.float32),
        lax.psum(group_up.astype(jnp.bfloat16), "rep").astype(jnp.float32),
        lax.psum(group_down.astype(jnp.bfloat16), "rep").astype(jnp.float32),
        lax.psum(group_norm.astype(jnp.bfloat16), "rep").astype(jnp.float32),
        lax.psum(grad_conv.astype(jnp.bfloat16), "rep").astype(jnp.float32),
    )
    local_sq = (
        jnp.sum(shard_qkv * shard_qkv)
        + jnp.sum(shard_out * shard_out)
        + jnp.sum(shard_up * shard_up)
        + jnp.sum(shard_down * shard_down)
        + jnp.sum(shard_norm * shard_norm)
    )
    total_sq, conv_total = lax.psum((local_sq, conv_rep), ("seq", "grp"))
    grad_total = jnp.sqrt(total_sq + jnp.sum(conv_total * conv_total))
    clip_factor = MAX_NORM / jnp.maximum(grad_total, MAX_NORM)
    qkv_new = adamw(
        qkv_weight, qkv_first, qkv_second, shard_qkv, clip_factor, RATE_MATRIX, DECAY_RATE
    )
    out_new = adamw(
        out_weight, out_first, out_second, shard_out, clip_factor, RATE_MATRIX, DECAY_RATE
    )
    up_new = adamw(up_weight, up_first, up_second, shard_up, clip_factor, RATE_MATRIX, DECAY_RATE)
    down_new = adamw(
        down_weight, down_first, down_second, shard_down, clip_factor, RATE_MATRIX, DECAY_RATE
    )
    norm_new = adamw(norm_params, norm_first, norm_second, shard_norm, clip_factor, RATE_NORM, 0.0)
    conv_new = adamw(conv_kernel, conv_first, conv_second, conv_total, clip_factor, RATE_CONV, 0.0)
    return (
        result.astype(jnp.bfloat16),
        input_grad,
        grad_total,
        qkv_new[0],
        qkv_new[1],
        qkv_new[2],
        out_new[0],
        out_new[1],
        out_new[2],
        up_new[0],
        up_new[1],
        up_new[2],
        down_new[0],
        down_new[1],
        down_new[2],
        norm_new[0],
        norm_new[1],
        norm_new[2],
        conv_new[0],
        conv_new[1],
        conv_new[2],
    )


def solution(mesh):
    in_specs = (
        P(("rep", "seq", "grp"), None),
        P(("rep", "seq", "grp"), None),
        P("rep", None),
        P(("seq", "grp"), None),
        P(("seq", "grp"), None),
        P(("seq", "grp"), None),
        P(("seq", "grp"), None),
        P(("seq", "grp"), None),
        P(("seq", "grp"), None),
        P(("seq", "grp"), None),
        P(("seq", "grp"), None),
        P(("seq", "grp"), None),
        P(("seq", "grp"), None),
        P(("seq", "grp"), None),
        P(("seq", "grp"), None),
        P(None, ("seq", "grp")),
        P(None, ("seq", "grp")),
        P(None, ("seq", "grp")),
        P(),
        P(),
        P(),
    )
    out_specs = (
        P(("rep", "seq", "grp"), None),
        P(("rep", "seq", "grp"), None),
        P(),
        P(("seq", "grp"), None),
        P(("seq", "grp"), None),
        P(("seq", "grp"), None),
        P(("seq", "grp"), None),
        P(("seq", "grp"), None),
        P(("seq", "grp"), None),
        P(("seq", "grp"), None),
        P(("seq", "grp"), None),
        P(("seq", "grp"), None),
        P(("seq", "grp"), None),
        P(("seq", "grp"), None),
        P(("seq", "grp"), None),
        P(None, ("seq", "grp")),
        P(None, ("seq", "grp")),
        P(None, ("seq", "grp")),
        P(),
        P(),
        P(),
    )
    return jax.shard_map(
        on_device, mesh=mesh, in_specs=in_specs, out_specs=out_specs, check_vma=False
    )
```

profile of v0, /device:TPU:0, one launch (start us, length us, event | category | flops | bytes accessed | tf_op | source)
XLA Modules:
  0.0 1063.3 jit_solution(4215209587072235914)
XLA Ops:
  11.2 43.3 %all-gather.6.cloned.1.call-done = bf16[768,2304]{1,0:T(8,128)(2,1)} async-done(((bf16[96,2304]{1,0:T(8,128)(2,1)}), bf16[768,2304]{1,0:T(8,128)(2,1)}) %all-gather.6.cloned.1.call-update) | async-done | bytes 3538960 | tf_op jit(solution)/shard_map/all_gather | solution.py:150
  61.7 58.8 %all-reduce.10.cloned.1.call-done = f32[256,1536]{1,0:T(8,128)} async-done(((f32[256,1536]{1,0:T(8,128)}), f32[256,1536]{1,0:T(8,128)}) %all-reduce.10.cloned.1.call-update) | async-done | bytes 1572880 | tf_op jit(solution)/shard_map/psum | solution.py:172
  137.2 9.8 all-gather
  151.2 3.8 collective-permute-start
  169.2 4.9 fusion.346
  201.6 28.3 %psum.100 = f32[4,64,12]{1,0,2:T(4,128)} all-reduce(f32[4,64,12]{1,0,2:T(4,128)} %div.271), channel_id=1, replica_groups=mesh['rep'=4,'seq'=4,'grp'=2] {'seq','grp'}, use_global_device_ids=true, to_apply=%region_7.8 | all-reduce | flops 3072 | bytes 24576 | tf_op jit(solution)/shard_map/psum | solution.py:188
  230.7 4.3 fusion.12
  258.7 4.6 fusion.67
  273.3 11.1 %fusion.114 = bf16[256,768]{1,0:T(8,128)(2,1)} fusion(f32[256,768]{1,0:T(8,128)} %copy.496, bf16[256,768]{1,0:T(8,128)(2,1)S(1)} %get-tuple-element.291, bf16[16,768]{1,0:T(8,128)(2,1)} %collective-permute-done.1, bf16[16,768]{1,0:T(8,128)(2,1)} %collective-permute-done, f32[256]{0:T(256)} %get-tuple-element.326, f32[768]{0:T(1024)S(1)} %get-tuple-element.208, ...), kind=kLoop, calls=%fused_computation.328 | loop fusion | flops 44826624 | bytes 1756160 | tf_op jit(solution)/shard_map/convert_element_type | solution.py:218
  288.7 11.8 %multiply_convert_fusion = (bf16[256,3072]{1,0:T(8,128)(2,1)}, f32[256,3072]{1,0:T(8,128)}, f32[256,3072]{1,0:T(8,128)}) fusion(bf16[768,3072]{1,0:T(8,128)(2,1)} %all-gather.10.cloned.1.call-done, f32[256,768]{1,0:T(8,128)} %copy-done.48, f32[768]{0:T(1024)S(1)} %get-tuple-element.242, f32[768]{0:T(1024)S(1)} %get-tuple-element.243, f32[256]{0:T(256)} %fusion.314, ...), kind=kOutput, calls=%fused_computation.49 | convolution fusion | flops 1260060672 | bytes 13377536 | tf_op jit(solution)/shard_map/dot_general | solution.py:224
  300.6 19.7 %all-gather.12.cloned.1.call-done = bf16[3072,768]{1,0:T(8,128)(2,1)} async-done(((bf16[384,768]{1,0:T(8,128)(2,1)}), bf16[3072,768]{1,0:T(8,128)(2,1)}) %all-gather.12.cloned.1.call-update) | async-done | bytes 4718608 | tf_op jit(solution)/shard_map/all_gather | solution.py:153
  320.3 4.7 fusion.370
  338.1 3.9 convolution_bitcast_fusion.3
  351.0 3.8 fusion.5
  357.5 54.3 %all-reduce.14.cloned.1.call-done = f32[4,12,64,64]{2,3,1,0:T(8,128)} async-done(((f32[4,12,64,64]{2,3,1,0:T(8,128)}), f32[4,12,64,64]{2,3,1,0:T(8,128)}) %all-reduce.14.cloned.1.call-update) | async-done | bytes 786448 | tf_op jit(solution)/shard_map/psum | solution.py:273
  411.8 5.7 fusion.43
  425.4 4.3 fusion.2
  447.4 3.8 convolution_multiply_fusion.1
  601.5 10.0 fusion.222
  616.0 4.1 convolution_bitcast_fusion
  620.1 8.0 copy.582
  629.8 5.4 fusion.335
  636.8 5.1 fusion.332
  739.6 65.0 %reduce-scatter.12.cloned.1.call-done = f32[96,3072]{1,0:T(8,128)} async-done(((f32[768,3072]{1,0:T(8,128)}), f32[96,3072]{1,0:T(8,128)}) %reduce-scatter.12.cloned.1.call-update) | async-done | bytes 1179664 | tf_op jit(solution)/shard_map/reduce_scatter | solution.py:316
  806.8 97.9 %reduce-scatter.14.cloned.1.call-done = f32[384,768]{1,0:T(8,128)} async-done(((f32[3072,768]{1,0:T(8,128)}), f32[384,768]{1,0:T(8,128)}) %reduce-scatter.14.cloned.1.call-update) | async-done | bytes 1179664 | tf_op jit(solution)/shard_map/reduce_scatter | solution.py:317
  921.0 15.5 %reduce-scatter.18.cloned.1.call-done = f32[96,4]{1,0:T(8,128)} async-done(((f32[768,4]{1,0:T(8,128)}), f32[96,4]{1,0:T(8,128)}) %reduce-scatter.18.cloned.1.call-update) | async-done | bytes 1552
  937.4 10.1 all-reduce.2
  948.2 4.1 fusion.68
  952.3 54.8 %all-reduce.18.cloned.1.call-done = (bf16[96,2304]{0,1:T(8,128)(2,1)}, bf16[96,768]{1,0:T(8,128)(2,1)}, bf16[96,3072]{1,0:T(8,128)(2,1)}, bf16[384,768]{1,0:T(8,128)(2,1)}) async-done(((bf16[96,2304]{0,1:T(8,128)(2,1)}, bf16[96,768]{1,0:T(8,128)(2,1)}, bf16[96,3072]{1,0:T(8,128)(2,1)}, bf16[384,768]{1,0:T(8,128)(2,1)}), (bf16[96,2304]{0,1:T(8,128)(2,1)}, bf16[96,768]{1,0:T(8,128)(2,1)}, ...) | async-done | bytes 1769488 | tf_op jit(solution)/shard_map/psum | solution.py:321
  1016.9 17.3 %all-reduce = (f32[]{:T(128)}, f32[12,33]{1,0:T(8,128)S(1)}) all-reduce(f32[]{:T(128)S(6)} %add.533, bf16[12,33]{1,0:T(8,128)(2,1)S(1)} %get-tuple-element.251), channel_id=1, replica_groups=mesh['rep'=4,'seq'=4,'grp'=2] {'seq','grp'}, use_global_device_ids=true, to_apply=%region_46.47 | all-reduce | flops 397 | bytes 2384 | tf_op jit(solution)/shard_map/psum | solution.py:335
  1036.2 3.8 multiply_subtract_fusion.2
  1047.5 3.8 multiply_subtract_fusion.1
  (746 shorter events, 454.1 us)
Async XLA Ops:
  7.2 47.3 %copy-start.93 = (bf16[256,768]{1,0:T(8,128)(2,1)S(1)}, bf16[256,768]{1,0:T(8,128)(2,1)}, u32[]{:S(2)}) copy-start(bf16[256,768]{1,0:T(8,128)(2,1)} %param.21) | copy-start | bytes 1179652
  7.2 47.3 %all-gather.6.cloned.1.call-start = ((), (), s32[]{:S(2)}) async-start(), calls=%async_computation.5 | async-start | bytes 3981312 | tf_op jit(solution)/shard_map/all_gather | solution.py:150
  9.3 111.1 %all-reduce.10.cloned.1.call-start = ((), (), s32[]{:S(2)}) async-start(), calls=%async_computation.6 | async-start | bytes 3145728 | tf_op jit(solution)/shard_map/psum | solution.py:172
  11.1 46.5 %copy-start.197 = (s32[256]{0:T(256)}, s32[256]{0:T(256)S(1)}, u32[]{:S(2)}) copy-start(s32[256]{0:T(256)S(1)} %slice.586) | copy-start | bytes 3076
  59.3 199.4 %all-reduce.12.cloned.1.call-start = ((), (), s32[]{:S(2)}) async-start(), calls=%async_computation.7 | async-start | bytes 3145728 | tf_op jit(solution)/shard_map/psum | solution.py:188
  59.5 60.9 %copy-start.195 = (f32[256]{0:T(256)}, f32[256]{0:T(256)S(1)}, u32[]{:S(2)}) copy-start(f32[256]{0:T(256)S(1)} %convert_element_type.489) | copy-start | bytes 3076
  60.5 63.9 %copy-start.52 = (f32[256,256]{0,1:T(8,128)}, f32[256,256]{0,1:T(8,128)S(1)}, u32[]{:S(2)}) copy-start(f32[256,256]{0,1:T(8,128)S(1)} %get-tuple-element.328) | copy-start | bytes 786436
  61.5 62.9 %copy-start.70 = (bf16[256,768]{0,1:T(8,128)(2,1)}, bf16[256,768]{0,1:T(8,128)(2,1)S(1)}, u32[]{:S(2)}) copy-start(bf16[256,768]{0,1:T(8,128)(2,1)S(1)} %copy.475) | copy-start | bytes 1179652
  61.6 61.3 %copy-start.71 = (bf16[256,768]{0,1:T(8,128)(2,1)}, bf16[256,768]{0,1:T(8,128)(2,1)S(1)}, u32[]{:S(2)}) copy-start(bf16[256,768]{0,1:T(8,128)(2,1)S(1)} %copy.476) | copy-start | bytes 1179652
  122.9 32.1 %copy-start.56 = (bf16[256,768]{0,1:T(8,128)(2,1)}, bf16[256,768]{0,1:T(8,128)(2,1)S(1)}, u32[]{:S(2)}) copy-start(bf16[256,768]{0,1:T(8,128)(2,1)S(1)} %copy.477) | copy-start | bytes 1179652
  128.9 155.5 %all-gather.8.cloned.1.call-start = ((), (), s32[]{:S(2)}) async-start(), calls=%async_computation.8 | async-start | bytes 1327104 | tf_op jit(solution)/shard_map/all_gather | solution.py:151
  130.5 158.2 %all-gather.10.cloned.1.call-start = ((), (), s32[]{:S(2)}) async-start(), calls=%async_computation.9 | async-start | bytes 5308416 | tf_op jit(solution)/shard_map/all_gather | solution.py:152
  131.5 188.8 %all-gather.12.cloned.1.call-start = ((), (), s32[]{:S(2)}) async-start(), calls=%async_computation.10 | async-start | bytes 5308416 | tf_op jit(solution)/shard_map/all_gather | solution.py:153
  132.5 279.3 %all-reduce.14.cloned.1.call-start = ((), (), s32[]{:S(2)}) async-start(), calls=%async_computation.11 | async-start | bytes 3145728 | tf_op jit(solution)/shard_map/psum | solution.py:273
  132.5 41.6 %copy-start.59 = (f32[64,64]{1,0:T(8,128)}, f32[64,64]{1,0:T(8,128)S(1)}, u32[]{:S(2)}) copy-start(f32[64,64]{1,0:T(8,128)S(1)} %fusion.297) | copy-start | bytes 49156
  132.6 41.5 %copy-start.90 = (f32[64,64]{1,0:T(8,128)}, f32[64,64]{1,0:T(8,128)S(1)}, u32[]{:S(2)}) copy-start(f32[64,64]{1,0:T(8,128)S(1)} %fusion.298) | copy-start | bytes 49156
  132.6 43.3 %copy-start.87 = (f32[64,64]{1,0:T(8,128)}, f32[64,64]{1,0:T(8,128)S(1)}, u32[]{:S(2)}) copy-start(f32[64,64]{1,0:T(8,128)S(1)} %fusion.299) | copy-start | bytes 49156
  149.9 123.4 %collective-permute-start.1 = (bf16[16,768]{1,0:T(8,128)(2,1)}, bf16[16,768]{1,0:T(8,128)(2,1)}, u32[]{:S(2)}, u32[]{:S(2)}) collective-permute-start(bf16[16,768]{1,0:T(8,128)(2,1)} %get-tuple-element.288), channel_id=1, source_target_pairs={{1,0},{2,1},{3,2},{4,3},{5,4},{6,5},{7,6},{9,8},{10,9},{11,10},{12... | collective-permute-start | bytes 73736 | tf_op jit(solution)/shard_map/ppermute | solution.py:40
  151.2 122.1 %collective-permute-start = (bf16[16,768]{1,0:T(8,128)(2,1)}, bf16[16,768]{1,0:T(8,128)(2,1)}, u32[]{:S(2)}, u32[]{:S(2)}) collective-permute-start(bf16[16,768]{1,0:T(8,128)(2,1)} %get-tuple-element.287), channel_id=1, source_target_pairs={{0,1},{1,2},{2,3},{3,4},{4,5},{5,6},{6,7},{8,9},{9,10},{10,11},{11... | collective-permute-start | bytes 73736 | tf_op jit(solution)/shard_map/ppermute | solution.py:38
  350.7 260.8 %all-reduce.16.cloned.1.call-start = ((), (), s32[]{:S(2)}) async-start(), calls=%async_computation.17 | async-start | bytes 3145728 | tf_op jit(solution)/shard_map/psum | solution.py:273
  432.2 303.6 %reduce-scatter.10.cloned.1.call-start = ((), (), s32[]{:S(2)}) async-start(), calls=%async_computation.12 | async-start | bytes 2654208 | tf_op jit(solution)/shard_map/reduce_scatter | solution.py:315
  433.6 167.5 %collective-permute-start.3 = (bf16[16,768]{1,0:T(8,128)(2,1)}, bf16[16,768]{1,0:T(8,128)(2,1)}, u32[]{:S(2)}, u32[]{:S(2)}) collective-permute-start(bf16[16,768]{1,0:T(8,128)(2,1)} %get-tuple-element.294), channel_id=1, source_target_pairs={{1,0},{2,1},{3,2},{4,3},{5,4},{6,5},{7,6},{9,8},{10,9},{11,10},{12... | collective-permute-start | bytes 73736 | tf_op jit(solution)/shard_map/ppermute | solution.py:40
  434.9 166.2 %collective-permute-start.2 = (bf16[16,768]{1,0:T(8,128)(2,1)}, bf16[16,768]{1,0:T(8,128)(2,1)}, u32[]{:S(2)}, u32[]{:S(2)}) collective-permute-start(bf16[16,768]{1,0:T(8,128)(2,1)} %get-tuple-element.293), channel_id=1, source_target_pairs={{0,1},{1,2},{2,3},{3,4},{4,5},{5,6},{6,7},{8,9},{9,10},{10,11},{11... | collective-permute-start | bytes 73736 | tf_op jit(solution)/shard_map/ppermute | solution.py:38
  446.9 290.4 %reduce-scatter.16.cloned.1.call-start = ((), (), s32[]{:S(2)}) async-start(), calls=%async_computation.15 | async-start | bytes 7962624
  628.1 176.5 %reduce-scatter.12.cloned.1.call-start = ((), (), s32[]{:S(2)}) async-start(), calls=%async_computation.13 | async-start | bytes 10616832 | tf_op jit(solution)/shard_map/reduce_scatter | solution.py:316
  635.2 269.6 %reduce-scatter.14.cloned.1.call-start = ((), (), s32[]{:S(2)}) async-start(), calls=%async_computation.14 | async-start | bytes 10616832 | tf_op jit(solution)/shard_map/reduce_scatter | solution.py:317
  641.9 294.7 %reduce-scatter.18.cloned.1.call-start = ((), (), s32[]{:S(2)}) async-start(), calls=%async_computation.16 | async-start | bytes 442368
  673.8 44.9 %copy-start.167 = (f32[256]{0:T(256)S(1)}, f32[256]{0:T(256)}, u32[]{:S(2)}) copy-start(f32[256]{0:T(256)} %get-tuple-element.296) | copy-start | bytes 3076
  691.4 40.8 %copy-start.178 = (f32[768]{0:T(1024)S(1)}, f32[768]{0:T(1024)}, u32[]{:S(2)}) copy-start(f32[768]{0:T(1024)} %get-tuple-element.187) | copy-start | bytes 9220
  718.7 288.4 %all-reduce.18.cloned.1.call-start = ((), (), s32[]{:S(2)}) async-start(), calls=%async_computation.18 | async-start | bytes 3833856 | tf_op jit(solution)/shard_map/psum | solution.py:321
  906.9 41.3 %copy-start.96 = (bf16[256,768]{1,0:T(8,128)(2,1)S(1)}, bf16[256,768]{1,0:T(8,128)(2,1)}, u32[]{:S(2)}) copy-start(bf16[256,768]{1,0:T(8,128)(2,1)} %copy-done.95) | copy-start | bytes 1179652
  906.9 41.3 %copy-start.98 = (bf16[256,768]{1,0:T(8,128)(2,1)S(1)}, bf16[256,768]{1,0:T(8,128)(2,1)}, u32[]{:S(2)}) copy-start(bf16[256,768]{1,0:T(8,128)(2,1)} %copy-done.97) | copy-start | bytes 1179652
  (198 other events, 741.8 us)
Sparse Core Ops, SparseCore 0:
  10.3 44.2 all-gather.5
  59.5 60.9 all-reduce.9
  129.0 61.2 all-reduce.11
  192.3 21.7 all-gather.7
  216.2 51.4 all-gather.9
  269.7 50.5 all-gather.11
  350.8 60.9 all-reduce.13
  432.3 61.0 all-reduce.15
  495.7 35.6 reduce-scatter.9
  628.3 76.1 reduce-scatter.15
  706.8 97.8 reduce-scatter.11
  806.8 97.8 reduce-scatter.13
  907.6 28.9 reduce-scatter.17
  941.5 65.5 all-reduce.17
where the time goes:
time: 1070 us; the launch traced here: 1060 us
  waiting for transfers between devices  410 us (38%)
  matrix products  288 us (27%)
  local copies, waits for them, and re-layouts  178 us (17%)
  other arithmetic  87.6 us (8%)
  blocking collectives  65.5 us (6%)
  between operations  23.3 us (2%)
  starting transfers between devices  11.4 us (1%)
    reduce_scatter x1, waiting for transfers between devices, on_device(): lax.psum_scatter(grad_down, ('seq', 'grp'), scatter_dimension=0, tiled=True)  97.9 us
    dot_general x36, matrix products, mixing_rest(): jnp.einsum('ahjk,ahkl->ahjl', product, inner, precision=HIGHEST_PREC)  88.9 us
    unnamed x467, local copies, waits for them, and re-layouts  83 us
    reduce_scatter x1, waiting for transfers between devices, on_device(): lax.psum_scatter(grad_up, ('seq', 'grp'), scatter_dimension=0, tiled=True)  65 us
    psum x1, waiting for transfers between devices, on_device(): lax.psum(contract_rows(col_hot, proj_low[:, :2 * D]), ('seq', 'grp'))  58.8 us
    psum x1, waiting for transfers between devices, on_device(): lax.psum(group_qkv.astype(jnp.bfloat16), 'rep').astype(jnp.float32)  54.8 us
    psum x2, waiting for transfers between devices, on_device(): lax.psum((d_mixed_part, d_meank_part), ('seq', 'grp'))  54.3 us
    dot_general x18, matrix products, mixing_rest(): jnp.einsum('ahjk,ahkl->ahjl', kernel_two, inverse, precision=HIGHEST_PREC)  49 us
  transfers between devices with their start and end apart: 18, of which 9 were waited for; matrix products, arithmetic and copies ran while one was open for 42% of the time, Pallas kernels for 0%

commit v1 on v0

--- a/solution.py
+++ b/solution.py
@@ -1,9 +1,12 @@
 import jax
 import jax.numpy as jnp
 from jax import lax
+from jax.experimental import pallas as pl
+from jax.experimental.pallas import tpu as pltpu
 from jax.sharding import PartitionSpec as P
 
 D = 768
+FF = 3072
 HEADS = 12
 HEAD = 64
 LAND = 64
@@ -13,8 +16,6 @@
 ITEMS = 4
 STEP = 10
 TOK_DEV = 256
-
-
 HIGHEST_PREC = lax.Precision.HIGHEST
 EPS_NORM = 1e-05
 BETA_ONE = 0.9
@@ -372,6 +373,704 @@
     )
 
 
+TOK = 256
+GRP_DEV = 8
+TEMPER = HEAD ** (-0.5)
+MESH_ID = pl.DeviceIdType.MESH
+BF = jnp.bfloat16
+F32 = jnp.float32
+EXT = 384
+
+
+def nn(left, right):
+    return jnp.dot(left, right, preferred_element_type=F32)
+
+
+def nt(left, right):
+    return lax.dot_general(left, right, (((1,), (1,)), ((), ())), preferred_element_type=F32)
+
+
+def tn(left, right):
+    return lax.dot_general(left, right, (((0,), (0,)), ((), ())), preferred_element_type=F32)
+
+
+def iota(shape, dim):
+    return lax.broadcasted_iota(jnp.int32, shape, dim)
+
+
+def split(value):
+    high = value.astype(BF)
+    return high, (value - high.astype(F32)).astype(BF)
+
+
+def lane_head(shape):
+    return iota(shape, len(shape) - 1) // HEAD
+
+
+def block_diag(value):
+    width = value.shape[1]
+    heads = width // HEAD
+    tiled = jnp.concatenate([value] * heads, axis=0)
+    keep = (iota((width, width), 0) // HEAD) == (iota((width, width), 1) // HEAD)
+    return jnp.where(keep, tiled, jnp.zeros_like(tiled))
+
+
+def left_of(value):
+    high, low = split(value)
+    return jnp.concatenate([high, low], axis=0)
+
+
+def right_of(value):
+    high, low = split(value)
+    return block_diag(high), block_diag(low)
+
+
+def mm_parts(left, right):
+    rows = left.shape[0] // 2
+    both = nn(left, right[0])
+    return both[:rows] + both[rows:] + nn(left[:rows], right[1])
+
+
+def mm(left, right):
+    return mm_parts(left_of(left), right_of(right))
+
+
+def packed_eye(width):
+    return (iota((LAND, width), 0) == iota((LAND, width), 1) % HEAD).astype(F32)
+
+
+def head_total(row):
+    heads = lane_head(row.shape)
+    out = jnp.zeros_like(row)
+    for head in range(row.shape[1] // HEAD):
+        mine = heads == head
+        out = jnp.where(mine, jnp.sum(jnp.where(mine, row, 0.0), axis=1, keepdims=True), out)
+    return out
+
+
+def head_rows(value, reduce_fn, neutral):
+    heads = lane_head(value.shape)
+    out = jnp.zeros_like(value)
+    for head in range(value.shape[1] // HEAD):
+        mine = heads == head
+        out = jnp.where(mine, reduce_fn(jnp.where(mine, value, neutral), axis=1, keepdims=True), out)
+    return out
+
+
+def kernel_two(query_marks, key_marks):
+    scores = nt(query_marks, block_diag(key_marks)) * TEMPER
+    scores_t = nt(key_marks, block_diag(query_marks)) * TEMPER
+    expo = jnp.exp(scores - head_rows(scores, jnp.max, -jnp.inf))
+    plain = expo / head_rows(expo, jnp.sum, 0.0)
+    expo_t = jnp.exp(scores_t - jnp.max(scores_t, axis=0, keepdims=True))
+    flipped = expo_t / jnp.sum(expo_t, axis=0, keepdims=True)
+    return plain, flipped
+
+
+def newton(plains, flippeds, save):
+    eye = packed_eye(plains[0].shape[1])
+    lefts = [left_of(p) for p in plains]
+    invs = [
+        f / head_total(jnp.sum(f * f, axis=0, keepdims=True)) for f in flippeds
+    ]
+    for it in range(NS_STEPS):
+        prods = [mm_parts(a, right_of(z)) for a, z in zip(lefts, invs)]
+        plefts = [left_of(p) for p in prods]
+        twos = [15.0 * eye - mm_parts(a, right_of(7.0 * eye - p)) for a, p in zip(plefts, prods)]
+        threes = [13.0 * eye - mm_parts(a, right_of(t)) for a, t in zip(plefts, twos)]
+        for index in range(len(invs)):
+            save(it, index, invs[index], prods[index], twos[index], threes[index])
+        invs = [0.25 * mm(z, t) for z, t in zip(invs, threes)]
+    return invs
+
+
+def lens_of(len_ref):
+    l0, l1, l2, l3 = len_ref[0, 0], len_ref[0, 1], len_ref[0, 2], len_ref[0, 3]
+    return (l0, l1, l2, l3), (0, l0, l0 + l1, l0 + l1 + l2)
+
+
+def choose(item, values):
+    out = jnp.where(item == 0, values[0], values[1])
+    out = jnp.where(item == 2, values[2], out)
+    return jnp.where(item == 3, values[3], out)
+
+
+def column_edges(col, lens, starts):
+    item = col // LAND
+    seg = col % LAND
+    length = choose(item, lens)
+    start = choose(item, starts)
+    low_edge = start + ((seg * length + LAND - 1) >> 6)
+    high_edge = start + (((seg + 1) * length + LAND - 1) >> 6)
+    return low_edge, high_edge, start, start + length
+
+
+def item_of(pos, starts):
+    return (
+        (pos >= starts[1]).astype(jnp.int32)
+        + (pos >= starts[2]).astype(jnp.int32)
+        + (pos >= starts[3]).astype(jnp.int32)
+    )
+
+
+def pair_lanes(hp):
+    return slice(128 * hp, 128 * hp + 128)
+
+
+def both_heads(value):
+    first = iota(value.shape, 1) < HEAD
+    zero = jnp.zeros_like(value)
+    return jnp.concatenate([jnp.where(first, value, zero), jnp.where(first, zero, value)], axis=0)
+
+
+def pick_heads(value):
+    rows = value.shape[0] // 2
+    first = iota((rows, 128), 1) < HEAD
+    return jnp.where(first, value[:rows], value[rows:])
+
+
+def toeplitz(tap_row, same):
+    wide = jnp.broadcast_to(tap_row, (TOK, EXT))
+    return split(pltpu.roll(wide, 0, 1, stride=1, stride_axis=0) * same)
+
+
+def conv_pair(taps_ref, hp, same, ext_pair):
+    outs = []
+    for head in (2 * hp, 2 * hp + 1):
+        high, low = toeplitz(taps_ref[head : head + 1, :], same)
+        outs.append(nn(high, ext_pair) + nn(low, ext_pair))
+    first = iota((TOK, 128), 1) < HEAD
+    return jnp.where(first, outs[0], outs[1])
+
+
+def same_item(first_row, lens, starts, reverse=False):
+    shape = (TOK, EXT)
+    row = iota(shape, 0)
+    if reverse:
+        row = TOK - 1 - row
+    pos = first_row + row
+    other = first_row + iota(shape, 1) - HALO
+    total = starts[3] + lens[3]
+    inside = (other >= 0) & (other < total) & (item_of(pos, starts) == item_of(other, starts))
+    return inside.astype(F32)
+
+
+def group_peers(me):
+    for step in range(1, GRP_DEV):
+        yield step, lax.rem(me + step, GRP_DEV)
+
+
+def place(rep, index):
+    return (rep, index // 2, lax.rem(index, 2))
+
+
+def greet(rep, me):
+    barrier = pltpu.get_barrier_semaphore()
+    for _, other in group_peers(me):
+        pl.semaphore_signal(barrier, inc=1, device_id=place(rep, other), device_id_type=MESH_ID)
+    pl.semaphore_wait(barrier, GRP_DEV - 1)
+
+
+def push(src, dst, send_sem, recv_sem, device):
+    copy = pltpu.make_async_remote_copy(
+        src_ref=src, dst_ref=dst, send_sem=send_sem, recv_sem=recv_sem,
+        device_id=device, device_id_type=MESH_ID,
+    )
+    copy.start()
+    return copy
+
+
+def attend_kernel(
+    len_ref, x_ref, w_ref, taps_ref,
+    q_ref, k_ref, v_ref, qm_ref, km_ref, wm_ref, a_ref, ext_ref,
+    res_ref, vloc_ref, dloc_ref, resl_ref, vl_ref, dl_ref,
+    win, halo, nd_src, nd_buf, wml, bias_cp, bias_pc, num_s, den_s, probs,
+    win_s, win_r, halo_s, halo_r, nd_s, nd_r, wml_s, wml_r,
+):
+    rep, seq, grp = lax.axis_index("rep"), lax.axis_index("seq"), lax.axis_index("grp")
+    me = seq * 2 + grp
+    first_row = me * TOK
+    is_owner = (me >= 1) & (me <= 6)
+    lens, starts = lens_of(len_ref)
+    greet(rep, me)
+
+    for part, ref in enumerate((q_ref, k_ref, v_ref)):
+        ref[...] = nn(x_ref[...], w_ref[:, D * part : D * part + D]).astype(BF)
+
+    @pl.when(me < GRP_DEV - 1)
+    def _():
+        push(v_ref.at[pl.ds(TOK - HALO, HALO)], halo.at[0], halo_s.at[0], halo_r.at[0], place(rep, me + 1))
+
+    @pl.when(me > 0)
+    def _():
+        push(v_ref.at[pl.ds(0, HALO)], halo.at[1], halo_s.at[1], halo_r.at[1], place(rep, me - 1))
+
+    qk = jnp.concatenate([q_ref[...], k_ref[...]], axis=1)
+    shape = (COLS, TOK)
+    pos = first_row + iota(shape, 1)
+    lo, hi, begin, end = column_edges(iota(shape, 0), lens, starts)
+    hot = ((pos >= lo) & (pos < hi)).astype(BF)
+    bias_cp[...] = jnp.where((pos >= begin) & (pos < end), 0.0, -1e30)
+    wshape = (16, TOK)
+    seg_hi = lens_edge(iota((LAND, TOK), 0) + 1, lens[1], starts[1])
+    base = jnp.sum((seg_hi <= first_row).astype(jnp.int32).astype(F32), axis=0, keepdims=True).astype(jnp.int32)
+    seg_w = base + iota(wshape, 0)
+    wpos = first_row + iota(wshape, 1)
+    whot = (
+        (wpos >= lens_edge(seg_w, lens[1], starts[1]))
+        & (wpos < lens_edge(seg_w + 1, lens[1], starts[1]))
+        & (seg_w < LAND)
+    ).astype(BF)
+    wsum = nn(whot, qk)
+    seg_c = base[:, :128] + iota((16, 128), 0)
+    wcount = (lens_edge(seg_c + 1, lens[1], starts[1]) - lens_edge(seg_c, lens[1], starts[1])).astype(F32)
+    wcount = jnp.concatenate([wcount] * 12, axis=1)
+    win[me] = (wsum / wcount).astype(BF)
+    for step, other in group_peers(me):
+        push(win.at[me], win.at[me], win_s.at[step - 1], win_r.at[me], place(rep, other))
+
+    sums = nn(hot, qk)
+    clo, chi, _, _ = column_edges(iota((COLS, 128), 0), lens, starts)
+    counts = (chi - clo).astype(F32)
+    counts6 = jnp.concatenate([counts] * 6, axis=1)
+    qm_ref[...] = (sums[:, :D] / counts6).astype(BF)
+    km_ref[...] = (sums[:, D:] / counts6).astype(BF)
+
+    pshape = (TOK, COLS)
+    ppos = first_row + iota(pshape, 0)
+    _, _, pbegin, pend = column_edges(iota(pshape, 1), lens, starts)
+    bias_pc[...] = jnp.where((ppos >= pbegin) & (ppos < pend), 0.0, -1e30)
+
+    for step, other in group_peers(me):
+        pltpu.make_async_copy(win.at[other], win.at[other], win_r.at[other]).wait()
+    sshape = (LAND, 128)
+    lane_dev = iota((LAND, 128), 1) // 16
+    lane_w = iota((LAND, 128), 1) % 16
+    seg_end = lens_edge(iota((LAND, 128), 0) + 1, lens[1], starts[1])
+    bases = jnp.sum((seg_end <= lane_dev * TOK).astype(jnp.int32).astype(F32), axis=0, keepdims=True).astype(jnp.int32)
+    scatter = (iota(sshape, 0) == bases + lane_w).astype(BF)
+    long_rows = nn(scatter, win[...].reshape(128, 2 * D))
+    qm_ref[LAND : 2 * LAND, :] = long_rows[:, :D].astype(BF)
+    km_ref[LAND : 2 * LAND, :] = long_rows[:, D:].astype(BF)
+
+    ones_wide = jnp.ones((TOK, 128), BF)
+    ones_row = jnp.ones((8, TOK), BF)
+    for hp in range(6):
+        lanes = pair_lanes(hp)
+        marks = both_heads(qm_ref[:, lanes])
+        scores = nt(marks, k_ref[:, lanes]) * TEMPER
+        expo = jnp.exp(scores + jnp.concatenate([bias_cp[...]] * 2, axis=0)).astype(BF)
+        nd = nn(expo, jnp.concatenate([v_ref[:, lanes], ones_wide], axis=1))
+        num = pick_heads(nd[:, :128])
+        nd_src[hp, 0:LAND, :] = num[LAND : 2 * LAND]
+        nd_src[hp, LAND : LAND + 8, :] = nt(
+            ones_row, jnp.concatenate([expo[LAND : 2 * LAND], expo[COLS + LAND : COLS + 2 * LAND]], axis=0)
+        )
+        num_s[:, lanes] = num
+        den_s[:, lanes] = pick_heads(nd[:, 128:])
+    for owner in range(1, 7):
+        @pl.when(me == owner)
+        def _():
+            nd_buf[owner] = nd_src[owner - 1]
+
+        @pl.when(me != owner)
+        def _():
+            push(nd_src.at[owner - 1], nd_buf.at[me], nd_s.at[owner - 1], nd_r.at[me], place(rep, owner))
+
+    wm_ref[...] = jnp.zeros_like(wm_ref)
+    n_local = jnp.where(me == 0, 1, jnp.where(me == GRP_DEV - 1, 2, 0))
+
+    def local_item(slot, carry):
+        row = jnp.where(me == 0, 0, 2 * LAND + slot * LAND)
+        rows = pl.ds(pl.multiple_of(row, LAND), LAND)
+        plains, flippeds = [], []
+        for part in range(3):
+            lanes = slice(256 * part, 256 * part + 256)
+            plain, flipped = kernel_two(qm_ref[rows, lanes], km_ref[rows, lanes])
+            plains.append(plain)
+            flippeds.append(flipped)
+
+        def save(it, index, *mats):
+            for m, mat in enumerate(mats):
+                res_ref[slot, index, it, m] = mat
+
+        invs = newton(plains, flippeds, save)
+        for part in range(3):
+            lanes = slice(256 * part, 256 * part + 256)
+            den = den_s[rows, lanes]
+            val = num_s[rows, lanes] / den
+            vloc_ref[slot, :, lanes] = val
+            dloc_ref[slot, :, lanes] = den
+            wm_ref[rows, lanes] = mm(invs[part], val).astype(BF)
+        return carry
+
+    lax.fori_loop(0, n_local, local_item, 0)
+
+    @pl.when(is_owner)
+    def _():
+        lanes = pl.ds(pl.multiple_of((me - 1) * 128, 128), 128)
+        plain, flipped = kernel_two(qm_ref[LAND : 2 * LAND, lanes], km_ref[LAND : 2 * LAND, lanes])
+
+        def save(it, index, *mats):
+            for m, mat in enumerate(mats):
+                resl_ref[it, m] = mat
+
+        (inv,) = newton([plain], [flipped], save)
+        for step, other in group_peers(me):
+            pltpu.make_async_copy(nd_buf.at[other], nd_buf.at[other], nd_r.at[other]).wait()
+        total = nd_buf[0]
+        for j in range(1, GRP_DEV):
+            total = total + nd_buf[j]
+        row = total[LAND : LAND + 1, :]
+        other_row = pltpu.roll(row, HEAD, 1)
+        spread = jnp.where(iota((128, 128), 0) < HEAD, row, other_row)
+        den = jnp.transpose(spread)[:LAND]
+        val = total[:LAND] / den
+        vl_ref[...] = val
+        dl_ref[...] = den
+        wml[me - 1] = mm(inv, val).astype(BF)
+        for step, other in group_peers(me):
+            push(wml.at[me - 1], wml.at[me - 1], wml_s.at[step - 1], wml_r.at[me - 1], place(rep, other))
+
+    for hp in range(6):
+        lanes = pair_lanes(hp)
+        scores = nt(q_ref[:, lanes], both_heads(km_ref[:, lanes])) * TEMPER
+        for half in range(2):
+            expo = jnp.exp(scores[:, COLS * half : COLS * half + COLS] + bias_pc[...])
+            probs[hp, :, COLS * half : COLS * half + COLS] = (
+                expo / jnp.sum(expo, axis=1, keepdims=True)
+            ).astype(BF)
+
+    @pl.when(me > 0)
+    def _():
+        pltpu.make_async_copy(halo.at[0], halo.at[0], halo_r.at[0]).wait()
+        ext_ref[0:HALO] = halo[0]
+
+    @pl.when(me == 0)
+    def _():
+        ext_ref[0:HALO] = jnp.zeros((HALO, D), BF)
+
+    @pl.when(me < GRP_DEV - 1)
+    def _():
+        pltpu.make_async_copy(halo.at[1], halo.at[1], halo_r.at[1]).wait()
+        ext_ref[HALO + TOK : 2 * HALO + TOK] = halo[1]
+
+    @pl.when(me == GRP_DEV - 1)
+    def _():
+        ext_ref[HALO + TOK : 2 * HALO + TOK] = jnp.zeros((HALO, D), BF)
+
+    ext_ref[HALO : HALO + TOK] = v_ref[...]
+    ext_ref[2 * HALO + TOK :] = jnp.zeros((EXT - TOK - 2 * HALO, D), BF)
+    same = same_item(first_row, lens, starts)
+
+    for owner in range(1, 7):
+        @pl.when(me != owner)
+        def _():
+            pltpu.make_async_copy(wml.at[owner - 1], wml.at[owner - 1], wml_r.at[owner - 1]).wait()
+
+        wm_ref[LAND : 2 * LAND, pair_lanes(owner - 1)] = wml[owner - 1]
+    for hp in range(6):
+        lanes = pair_lanes(hp)
+        att = nn(probs[hp], both_heads(wm_ref[:, lanes]))
+        a_ref[:, lanes] = (att + conv_pair(taps_ref, hp, same, ext_ref[:, lanes])).astype(BF)
+
+    for step, other in group_peers(me):
+        pltpu.make_async_copy(win.at[me], win.at[me], win_s.at[step - 1]).wait()
+    for owner in range(1, 7):
+        @pl.when(me != owner)
+        def _():
+            pltpu.make_async_copy(nd_src.at[owner - 1], nd_src.at[owner - 1], nd_s.at[owner - 1]).wait()
+
+    @pl.when(is_owner)
+    def _():
+        for step, other in group_peers(me):
+            pltpu.make_async_copy(wml.at[0], wml.at[0], wml_s.at[step - 1]).wait()
+
+    @pl.when(me < GRP_DEV - 1)
+    def _():
+        pltpu.make_async_copy(halo.at[0], halo.at[0], halo_s.at[0]).wait()
+
+    @pl.when(me > 0)
+    def _():
+        pltpu.make_async_copy(halo.at[1], halo.at[1], halo_s.at[1]).wait()
+
+
+def lens_edge(seg, length, start):
+    return start + ((seg * length + LAND - 1) >> 6)
+
+
+COLS = ITEMS * LAND
+VM = pl.BlockSpec(memory_space=pltpu.VMEM)
+SM = pl.BlockSpec(memory_space=pltpu.SMEM)
+
+
+def attend(item_lengths, tokens, w_all, taps):
+    sds = jax.ShapeDtypeStruct
+    row = sds((TOK, D), BF)
+    outs = [row, row, row, row, row, row, row, sds((EXT, D), BF),
+            sds((2, 3, NS_STEPS, 4, LAND, 256), F32), sds((2, LAND, D), F32), sds((2, LAND, D), F32),
+            sds((NS_STEPS, 4, LAND, 128), F32), sds((LAND, 128), F32), sds((LAND, 128), F32)]
+    dma = pltpu.SemaphoreType.DMA
+    scratch = [
+        pltpu.VMEM((8, 16, 2 * D), BF), pltpu.VMEM((2, HALO, D), BF), pltpu.VMEM((6, LAND + 8, 128), F32),
+        pltpu.VMEM((8, LAND + 8, 128), F32), pltpu.VMEM((6, LAND, 128), BF),
+        pltpu.VMEM((COLS, TOK), F32), pltpu.VMEM((TOK, COLS), F32), pltpu.VMEM((COLS, D), F32),
+        pltpu.VMEM((COLS, D), F32), pltpu.VMEM((6, TOK, 2 * COLS), BF),
+        dma((7,)), dma((8,)), dma((2,)), dma((2,)), dma((6,)), dma((8,)), dma((7,)), dma((6,)),
+    ]
+    return pl.pallas_call(
+        attend_kernel, out_shape=outs, in_specs=[SM, VM, VM, VM], out_specs=[VM] * len(outs),
+        scratch_shapes=scratch, name="attend",
+        compiler_params=pltpu.CompilerParams(collective_id=1, has_side_effects=True, vmem_limit_bytes=56 * 2**20),
+    )(item_lengths, tokens, w_all, taps)
+
+
+def full_marks(marks):
+    index = lax.axis_index(("seq", "grp"))
+    rows = jnp.arange(ITEMS * LAND)[:, None]
+    keep = ((rows // LAND != 1) | (index == 0)).astype(jnp.bfloat16)
+    return lax.psum(marks * keep, ("seq", "grp"))
+
+
+def on_device_fast(
+    tokens,
+    cotangent,
+    item_lengths,
+    qkv_weight,
+    qkv_first,
+    qkv_second,
+    out_weight,
+    out_first,
+    out_second,
+    up_weight,
+    up_first,
+    up_second,
+    down_weight,
+    down_first,
+    down_second,
+    norm_params,
+    norm_first,
+    norm_second,
+    conv_kernel,
+    conv_first,
+    conv_second,
+):
+    temper = HEAD ** (-0.5)
+    col_total = ITEMS * LAND
+    w_qkv, w_out, w_up, w_down, gains_low = (
+        lax.all_gather(qkv_weight.astype(jnp.bfloat16), ("seq", "grp"), axis=0, tiled=True),
+        lax.all_gather(out_weight.astype(jnp.bfloat16), ("seq", "grp"), axis=0, tiled=True),
+        lax.all_gather(up_weight.astype(jnp.bfloat16), ("seq", "grp"), axis=0, tiled=True),
+        lax.all_gather(down_weight.astype(jnp.bfloat16), ("seq", "grp"), axis=0, tiled=True),
+        lax.all_gather(norm_params.astype(jnp.bfloat16), ("seq", "grp"), axis=1, tiled=True),
+    )
+    gains_all = gains_low.astype(jnp.float32)
+    lengths = item_lengths[0]
+    taps = jnp.pad(conv_kernel, ((0, 4), (0, EXT - KERNEL)))
+    queries, key_rows, value_rows, mean_q, mean_k, mixed_low, branch, value_pad = attend(
+        item_lengths, tokens, w_qkv, taps
+    )[:8]
+    value_ext = value_pad[: TOK_DEV + 2 * HALO]
+    first_row = lax.axis_index(("seq", "grp")) * TOK_DEV
+    positions = first_row - HALO + jnp.arange(TOK_DEV + 2 * HALO, dtype=jnp.int32)
+    item_ext, column_ext = locate(positions, lengths)
+    item_mid = item_ext[HALO : HALO + TOK_DEV]
+    column_mid = column_ext[HALO : HALO + TOK_DEV]
+    col_ids = jnp.arange(col_total, dtype=jnp.int32)
+    col_hot = (column_mid[:, None] == col_ids[None, :]).astype(jnp.bfloat16)
+    member = (item_mid[:, None] == (col_ids // LAND)[None, :]).astype(jnp.float32)
+    counts_f = landmark_counts(lengths).astype(jnp.float32)
+    mean_q, mean_k = full_marks(mean_q), full_marks(mean_k)
+    query_heads = queries.reshape(TOK_DEV, HEADS, HEAD)
+    key_heads = key_rows.reshape(TOK_DEV, HEADS, HEAD)
+    value_heads = value_rows.reshape(TOK_DEV, HEADS, HEAD)
+    mean_q3 = mean_q.reshape(col_total, HEADS, HEAD)
+    mean_k3 = mean_k.reshape(col_total, HEADS, HEAD)
+    scores_key = (
+        jnp.einsum("chd,phd->chp", mean_q3, key_heads, preferred_element_type=jnp.float32) * temper
+    )
+    expo_key = jnp.exp(scores_key) * jnp.transpose(member)[:, None, :]
+    expo_low = expo_key.astype(jnp.bfloat16)
+    num_part = jnp.einsum(
+        "chp,phd->chd", expo_low, value_heads, preferred_element_type=jnp.float32
+    ).reshape(col_total, D)
+    num_all, den_all = lax.psum((num_part, jnp.sum(expo_key, axis=2)), ("seq", "grp"))
+    query_marks4 = mean_q.reshape(ITEMS, LAND, HEADS, HEAD)
+    key_marks4 = mean_k.reshape(ITEMS, LAND, HEADS, HEAD)
+    mark_scores = (
+        jnp.einsum("ajhd,akhd->ahjk", query_marks4, key_marks4, preferred_element_type=jnp.float32)
+        * temper
+    )
+    mixed_rows, mix_pull = jax.vjp(mixing_rest, mark_scores, num_all, den_all)
+    mixed3 = mixed_rows.astype(jnp.bfloat16).reshape(col_total, HEADS, HEAD)
+    scores_tok = (
+        jnp.einsum("phd,chd->phc", query_heads, mean_k3, preferred_element_type=jnp.float32)
+        * temper
+    )
+    expo_tok = jnp.exp(scores_tok) * member[:, None, :]
+    attn_probs = expo_tok / jnp.sum(expo_tok, axis=2, keepdims=True)
+    probs_low = attn_probs.astype(jnp.bfloat16)
+    channel_taps = jnp.repeat(conv_kernel, HEAD, axis=0)
+    same_masks = [
+        (item_ext[offset : offset + TOK_DEV] == item_mid).astype(jnp.float32)
+        for offset in range(KERNEL)
+    ]
+    attn_out = jnp.dot(branch, w_out, preferred_element_type=jnp.float32)
+    normed_one, norm_one_pull = jax.vjp(
+        layer_norm, tokens.astype(jnp.float32) + attn_out, gains_all[0], gains_all[1]
+    )
+    normed_low = normed_one.astype(jnp.bfloat16)
+    up_out = jnp.dot(normed_low, w_up, preferred_element_type=jnp.float32)
+    activated, gelu_pull = jax.vjp(gelu_exact, up_out)
+    act_low = activated.astype(jnp.bfloat16)
+    down_out = jnp.dot(act_low, w_down, preferred_element_type=jnp.float32)
+    result, norm_two_pull = jax.vjp(layer_norm, normed_one + down_out, gains_all[2], gains_all[3])
+    d_hidden_two, d_gain_two, d_shift_two = norm_two_pull(cotangent.astype(jnp.float32))
+    d_down_low = d_hidden_two.astype(jnp.bfloat16)
+    grad_down = contract_rows(act_low, d_down_low)
+    (d_up,) = gelu_pull(contract_cols(d_down_low, w_down))
+    d_up_low = d_up.astype(jnp.bfloat16)
+    grad_up = contract_rows(normed_low, d_up_low)
+    d_normed = d_hidden_two + contract_cols(d_up_low, w_up)
+    d_hidden_one, d_gain_one, d_shift_one = norm_one_pull(d_normed)
+    d_attn_low = d_hidden_one.astype(jnp.bfloat16)
+    grad_out = contract_rows(branch, d_attn_low)
+    d_branch_low = contract_cols(d_attn_low, w_out).astype(jnp.bfloat16)
+    d_branch_f = d_branch_low.astype(jnp.float32)
+    d_branch_ext = extended(d_branch_low, ((("seq", "grp"), 0),), HALO)
+    d_values_conv = jnp.zeros((TOK_DEV, D), jnp.float32)
+    tap_grads = []
+    for offset in range(KERNEL):
+        d_values_conv = d_values_conv + d_branch_ext[offset : offset + TOK_DEV] * (
+            channel_taps[:, KERNEL - 1 - offset][None, :] * same_masks[offset][:, None]
+        )
+        tap_grads.append(
+            jnp.sum(
+                d_branch_f * value_ext[offset : offset + TOK_DEV] * same_masks[offset][:, None],
+                axis=0,
+            )
+        )
+    grad_conv = jnp.sum(jnp.stack(tap_grads, axis=1).reshape(HEADS, HEAD, KERNEL), axis=1)
+    d_attended = d_branch_low.reshape(TOK_DEV, HEADS, HEAD)
+    d_mixed_part = jnp.einsum(
+        "phc,phd->chd", probs_low, d_attended, preferred_element_type=jnp.float32
+    ).reshape(col_total, D)
+    d_probs = jnp.einsum("phd,chd->phc", d_attended, mixed3, preferred_element_type=jnp.float32)
+    d_scores_tok = (
+        attn_probs * (d_probs - jnp.sum(attn_probs * d_probs, axis=2, keepdims=True))
+    ).astype(jnp.bfloat16)
+    d_query_tok = (
+        jnp.einsum("phc,chd->phd", d_scores_tok, mean_k3, preferred_element_type=jnp.float32)
+        * temper
+    )
+    d_meank_part = (
+        jnp.einsum(
+            "phc,phd->chd", d_scores_tok, query_heads, preferred_element_type=jnp.float32
+        ).reshape(col_total, D)
+        * temper
+    )
+    d_mixed, d_meank_tok = lax.psum((d_mixed_part, d_meank_part), ("seq", "grp"))
+    d_mark_scores, d_num, d_den = mix_pull(d_mixed)
+    d_mark_scaled = d_mark_scores * temper
+    d_mean_q_mix = jnp.einsum(
+        "ahjk,akhd->ajhd", d_mark_scaled, key_marks4.astype(jnp.float32), precision=HIGHEST_PREC
+    ).reshape(col_total, D)
+    d_mean_k_mix = jnp.einsum(
+        "ahjk,ajhd->akhd", d_mark_scaled, query_marks4.astype(jnp.float32), precision=HIGHEST_PREC
+    ).reshape(col_total, D)
+    d_num3 = d_num.reshape(col_total, HEADS, HEAD)
+    d_expo = d_den[:, :, None] + jnp.einsum(
+        "chd,phd->chp", d_num3, value_heads.astype(jnp.float32), precision=HIGHEST_PREC
+    )
+    d_scores_key = (expo_key * d_expo).astype(jnp.bfloat16)
+    d_key_mix = (
+        jnp.einsum("chp,chd->phd", d_scores_key, mean_q3, preferred_element_type=jnp.float32)
+        * temper
+    )
+    d_meanq_part = (
+        jnp.einsum(
+            "chp,phd->chd", d_scores_key, key_heads, preferred_element_type=jnp.float32
+        ).reshape(col_total, D)
+        * temper
+    )
+    d_value_mix = jnp.einsum(
+        "chp,chd->phd", expo_low.astype(jnp.float32), d_num3, precision=HIGHEST_PREC
+    )
+    d_meanq_tok = lax.psum(d_meanq_part, ("seq", "grp"))
+    d_sums = (
+        jnp.concatenate([d_mean_q_mix + d_meanq_tok, d_mean_k_mix + d_meank_tok], axis=1)
+        / counts_f[:, None]
+    )
+    d_land_rows = jnp.dot(col_hot.astype(jnp.float32), d_sums, precision=HIGHEST_PREC)
+    d_queries = d_query_tok.reshape(TOK_DEV, D) + d_land_rows[:, :D]
+    d_keys = d_key_mix.reshape(TOK_DEV, D) + d_land_rows[:, D:]
+    d_values = d_value_mix.reshape(TOK_DEV, D) + d_values_conv
+    d_proj_low = jnp.concatenate([d_queries, d_keys, d_values], axis=1).astype(jnp.bfloat16)
+    grad_qkv = contract_rows(tokens, d_proj_low)
+    input_grad = (d_hidden_one + contract_cols(d_proj_low, w_qkv)).astype(jnp.bfloat16)
+    grad_norms = jnp.stack([d_gain_one, d_shift_one, d_gain_two, d_shift_two])
+    group_qkv, group_out, group_up, group_down, group_norm = (
+        lax.psum_scatter(grad_qkv, ("seq", "grp"), scatter_dimension=0, tiled=True),
+        lax.psum_scatter(grad_out, ("seq", "grp"), scatter_dimension=0, tiled=True),
+        lax.psum_scatter(grad_up, ("seq", "grp"), scatter_dimension=0, tiled=True),
+        lax.psum_scatter(grad_down, ("seq", "grp"), scatter_dimension=0, tiled=True),
+        lax.psum_scatter(grad_norms, ("seq", "grp"), scatter_dimension=1, tiled=True),
+    )
+    shard_qkv, shard_out, shard_up, shard_down, shard_norm, conv_rep = (
+        lax.psum(group_qkv.astype(jnp.bfloat16), "rep").astype(jnp.float32),
+        lax.psum(group_out.astype(jnp.bfloat16), "rep").astype(jnp.float32),
+        lax.psum(group_up.astype(jnp.bfloat16), "rep").astype(jnp.float32),
+        lax.psum(group_down.astype(jnp.bfloat16), "rep").astype(jnp.float32),
+        lax.psum(group_norm.astype(jnp.bfloat16), "rep").astype(jnp.float32),
+        lax.psum(grad_conv.astype(jnp.bfloat16), "rep").astype(jnp.float32),
+    )
+    local_sq = (
+        jnp.sum(shard_qkv * shard_qkv)
+        + jnp.sum(shard_out * shard_out)
+        + jnp.sum(shard_up * shard_up)
+        + jnp.sum(shard_down * shard_down)
+        + jnp.sum(shard_norm * shard_norm)
+    )
+    total_sq, conv_total = lax.psum((local_sq, conv_rep), ("seq", "grp"))
+    grad_total = jnp.sqrt(total_sq + jnp.sum(conv_total * conv_total))
+    clip_factor = MAX_NORM / jnp.maximum(grad_total, MAX_NORM)
+    qkv_new = adamw(
+        qkv_weight, qkv_first, qkv_second, shard_qkv, clip_factor, RATE_MATRIX, DECAY_RATE
+    )
+    out_new = adamw(
+        out_weight, out_first, out_second, shard_out, clip_factor, RATE_MATRIX, DECAY_RATE
+    )
+    up_new = adamw(up_weight, up_first, up_second, shard_up, clip_factor, RATE_MATRIX, DECAY_RATE)
+    down_new = adamw(
+        down_weight, down_first, down_second, shard_down, clip_factor, RATE_MATRIX, DECAY_RATE
+    )
+    norm_new = adamw(norm_params, norm_first, norm_second, shard_norm, clip_factor, RATE_NORM, 0.0)
+    conv_new = adamw(conv_kernel, conv_first, conv_second, conv_total, clip_factor, RATE_CONV, 0.0)
+    return (
+        result.astype(jnp.bfloat16),
+        input_grad,
+        grad_total,
+        qkv_new[0],
+        qkv_new[1],
+        qkv_new[2],
+        out_new[0],
+        out_new[1],
+        out_new[2],
+        up_new[0],
+        up_new[1],
+        up_new[2],
+        down_new[0],
+        down_new[1],
+        down_new[2],
+        norm_new[0],
+        norm_new[1],
+        norm_new[2],
+        conv_new[0],
+        conv_new[1],
+        conv_new[2],
+    )
+
+
 def solution(mesh):
     in_specs = (
         P(("rep", "seq", "grp"), None),
@@ -419,6 +1118,8 @@
         P(),
         P(),
     )
+    fast = dict(mesh.shape) == {"rep": 4, "seq": 4, "grp": 2}
+    body = on_device_fast if fast else on_device
     return jax.shard_map(
-        on_device, mesh=mesh, in_specs=in_specs, out_specs=out_specs, check_vma=False
-    )
+        body, mesh=mesh, in_specs=in_specs, out_specs=out_specs, check_vma=False
+    )

time: 1070 us -> 1050 us (0.981)
  local copies, waits for them, and re-layouts: 178 us -> 104 us
  waiting for transfers between devices: 410 us -> 459 us
  Pallas kernels: 0 us -> 41.5 us
  other arithmetic: 87.6 us -> 61.4 us
  matrix products: 288 us -> 276 us
    unnamed x16 -> x15, waiting for transfers between devices: 15.8 us -> 65.1 us
    pallas_call x0 -> x1, Pallas kernels: none -> 41.5 us  [attend(): pl.pallas_call(attend_kernel, out_shape=outs, in_specs=[SM, VM, VM, VM],...]
    another operation x34, local copies, waits for them, and re-layouts: 43.2 us -> 4.93 us  [on_device_fast(): jnp.stack(tap_grads, axis=1).reshape(HEADS, HEAD, KERNEL)]
    reduce_scatter x3, waiting for transfers between devices: 163 us -> 196 us  [the longest x1 98.2 us: on_device_fast(): lax.psum_scatter(grad_down, ('seq', 'grp'), scatter_dimension=0, tiled=True)]
    unnamed x467 -> x453, local copies, waits for them, and re-layouts: 83 us -> 51.4 us
    all_gather x4, waiting for transfers between devices: 63.1 us -> 43.8 us  [the longest x1 43.8 us: on_device_fast(): lax.all_gather(qkv_weight.astype(jnp.bfloat16), ('seq', 'grp'), axis=0, t...]
    convert_element_type x17 -> x16, other arithmetic: 31.2 us -> 14.9 us  [the longest x4 2.75 us: on_device_fast(): (item_ext[offset:offset + TOK_DEV] == item_mid).astype(jnp.float32)]
    psum x5 -> x4, waiting for transfers between devices: 168 us -> 154 us  [the longest x2 67.6 us: on_device_fast(): lax.psum((d_mixed_part, d_meank_part), ('seq', 'grp'))]
  transfers between devices with their start and end apart: 18 -> 15, of which waited for: 9 -> 8; matrix products, arithmetic and copies ran while one was open for 42% -> 32% of each run, Pallas kernels for 0% -> 4%
where the time goes in v1:
time: 1050 us; the launch traced here: 1040 us
  waiting for transfers between devices  459 us (44%)
  matrix products  276 us (26%)
  local copies, waits for them, and re-layouts  104 us (10%)
  blocking collectives  65.7 us (6%)
  other arithmetic  61.4 us (6%)
  Pallas kernels  41.5 us (4%)
  between operations  23.3 us (2%)
    reduce_scatter x1, waiting for transfers between devices, on_device_fast(): lax.psum_scatter(grad_down, ('seq', 'grp'), scatter_dimension=0, tiled=True)  98.2 us
    reduce_scatter x1, waiting for transfers between devices, on_device_fast(): lax.psum_scatter(grad_up, ('seq', 'grp'), scatter_dimension=0, tiled=True)  97.9 us
    dot_general x36, matrix products, mixing_rest(): jnp.einsum('ahjk,ahkl->ahjl', product, inner, precision=HIGHEST_PREC)  90.7 us
    psum x2, waiting for transfers between devices, on_device_fast(): lax.psum((d_mixed_part, d_meank_part), ('seq', 'grp'))  67.6 us
    unnamed x15, waiting for transfers between devices  65.1 us
    psum x1, waiting for transfers between devices, on_device_fast(): lax.psum(group_qkv.astype(jnp.bfloat16), 'rep').astype(jnp.float32)  54.5 us
    unnamed x453, local copies, waits for them, and re-layouts  51.4 us
    dot_general x18, matrix products, mixing_rest(): jnp.einsum('ahjk,ahkl->ahjl', kernel_two, inverse, precision=HIGHEST_PREC)  49.2 us
  transfers between devices with their start and end apart: 15, of which 8 were waited for; matrix products, arithmetic and copies ran while one was open for 32% of the time, Pallas kernels for 4%

profile of v1, /device:TPU:0, one launch (start us, length us, event | category | flops | bytes accessed | tf_op | source)
XLA Modules:
  0.0 1037.4 jit_solution(6500564781577511931)
XLA Ops:
  10.7 43.8 %all-gather.6.cloned.1.call-done.w_ref = bf16[768,2304]{1,0:T(8,128)(2,1)} async-done(((bf16[96,2304]{1,0:T(8,128)(2,1)}), bf16[768,2304]{1,0:T(8,128)(2,1)}) %all-gather.6.cloned.1.call-update) | async-done | bytes 3538960 | tf_op jit(solution)/shard_map/all_gather | solution.py:861
  54.5 41.5 %attend.1 = (bf16[256,768]{1,0:T(8,128)(2,1)}, bf16[256,768]{1,0:T(8,128)(2,1)}, bf16[256,768]{1,0:T(8,128)(2,1)}, bf16[256,768]{1,0:T(8,128)(2,1)}, bf16[256,76...) custom-call(s32[1,4]{1,0:T(1,128)} %len_ref.1, ...), custom_call_target="tpu_custom_call" | custom-call | tf_op jit(solution)/shard_map/attend/pallas_call | solution.py:821
  107.1 10.7 %all-gather = bf16[8,96,4]{1,2,0:T(4,128)(2,1)S(1)} all-gather(bf16[1,96,4]{1,2,0:T(4,128)(2,1)S(1)} %convert_bitcast_fusion), channel_id=1, replica_groups=mesh['rep'=4,'seq'=4,'grp'=2] {'seq','grp'}, dimensions={0}, use_global_device_ids=true | all-gather | bytes 6912 | tf_op jit(solution)/shard_map/all_gather | solution.py:865
  123.6 32.1 %all-reduce.16.cloned.1.call-done = (bf16[256,768]{1,0:T(8,128)(2,1)}, bf16[256,768]{1,0:T(8,128)(2,1)}) async-done(((bf16[256,768]{1,0:T(8,128)(2,1)}, bf16[256,768]{1,0:T(8,128)(2,1)}), (bf16[256,768]{1,0:T(8,128)(2,1)}, bf16[256,768]{1,0:T(8,128)(2,1)})) %all-reduce.16.cloned.1.call-update) | async-done | bytes 786448 | tf_op jit(solution)/shard_map/psum | solution.py:832
  167.0 27.5 %psum.108 = f32[4,64,12]{1,0,2:T(4,128)S(1)} all-reduce(f32[4,64,12]{1,0,2:T(4,128)S(1)} %div.270), channel_id=1, replica_groups=mesh['rep'=4,'seq'=4,'grp'=2] {'seq','grp'}, use_global_device_ids=true, to_apply=%region_15.16 | all-reduce | flops 3072 | bytes 24576 | tf_op jit(solution)/shard_map/psum | solution.py:897
  206.6 5.1 fusion.278
  260.6 11.9 %multiply_convert_fusion = (bf16[256,3072]{1,0:T(8,128)(2,1)}, f32[256,3072]{1,0:T(8,128)}, f32[256,3072]{1,0:T(8,128)}) fusion(bf16[768,3072]{1,0:T(8,128)(2,1)} %all-gather.10.cloned.1.call-done, f32[256,768]{1,0:T(8,128)S(1)} %get-tuple-element.345, f32[768]{0:T(1024)S(1)} %get-tuple-element.256, f32[768]{0:T(1024)S(1)} %get-tuple-element.257, ...), kind=kOutput, calls=%fused_computation.48 | convolution fusion | flops 1260060672 | bytes 13377536 | tf_op jit(solution)/shard_map/dot_general | solution.py:923
  272.4 4.4 fusion.295
  288.0 3.8 fusion.70
  297.5 3.7 convolution_subtract_fusion
  305.3 67.6 %all-reduce.14.cloned.1.call-done = (f32[4,12,64,64]{2,3,1,0:T(8,128)}, f32[4,64,12,64]{1,3,2,0:T(8,128)}) async-done(((f32[4,12,64,64]{2,3,1,0:T(8,128)}, f32[4,64,12,64]{1,3,2,0:T(8,128)}), (f32[4,12,64,64]{2,3,1,0:T(8,128)}, f32[4,64,12,64]{1,3,2,0:T(8,128)})) %all-reduce.14.cloned.1.call-update) | async-done | bytes 1572880 | tf_op jit(solution)/shard_map/psum | solution.py:972
  372.9 5.6 fusion.69
  378.4 3.5 fusion.43
  399.4 4.3 fusion.2
  408.1 3.6 collective-permute-start
  415.5 3.8 convolution_multiply_fusion.1
  545.6 3.6 multiply_reduce_fusion
  575.0 9.7 fusion.186
  589.3 4.1 convolution_bitcast_fusion
  593.4 8.0 copy.567
  602.8 5.4 fusion.268
  609.9 5.2 fusion.265
  635.7 43.0 %reduce-scatter.16.cloned.1.call-done = f32[96,2304]{1,0:T(8,128)} async-done(((f32[768,2304]{1,0:T(8,128)}), f32[96,2304]{1,0:T(8,128)}) %reduce-scatter.16.cloned.1.call-update) | async-done | bytes 884752
  680.9 97.9 %reduce-scatter.12.cloned.1.call-done = f32[96,3072]{1,0:T(8,128)} async-done(((f32[768,3072]{1,0:T(8,128)}), f32[96,3072]{1,0:T(8,128)}) %reduce-scatter.12.cloned.1.call-update) | async-done | bytes 1179664 | tf_op jit(solution)/shard_map/reduce_scatter | solution.py:1015
  781.0 98.2 %reduce-scatter.14.cloned.1.call-done = f32[384,768]{1,0:T(8,128)} async-done(((f32[3072,768]{1,0:T(8,128)}), f32[384,768]{1,0:T(8,128)}) %reduce-scatter.14.cloned.1.call-update) | async-done | bytes 1179664 | tf_op jit(solution)/shard_map/reduce_scatter | solution.py:1016
  889.1 21.8 %reduce-scatter.18.cloned.1.call-done = f32[96,4]{1,0:T(8,128)} async-done(((f32[768,4]{1,0:T(8,128)}), f32[96,4]{1,0:T(8,128)}) %reduce-scatter.18.cloned.1.call-update) | async-done | bytes 1552
  911.8 10.1 all-reduce.5
  922.6 4.2 fusion.73
  926.7 54.5 %all-reduce.18.cloned.1.call-done = (bf16[96,2304]{0,1:T(8,128)(2,1)}, bf16[96,768]{1,0:T(8,128)(2,1)}, bf16[96,3072]{1,0:T(8,128)(2,1)}, bf16[384,768]{1,0:T(8,128)(2,1)}) async-done(((bf16[96,2304]{0,1:T(8,128)(2,1)}, bf16[96,768]{1,0:T(8,128)(2,1)}, bf16[96,3072]{1,0:T(8,128)(2,1)}, bf16[384,768]{1,0:T(8,128)(2,1)}), (bf16[96,2304]{0,1:T(8,128)(2,1)}, bf16[96,768]{1,0:T(8,128)(2,1)}, ...) | async-done | bytes 1769488 | tf_op jit(solution)/shard_map/psum | solution.py:1020
  991.0 17.3 %all-reduce.1 = (f32[]{:T(128)}, f32[12,33]{1,0:T(8,128)S(1)}) all-reduce(f32[]{:T(128)S(6)} %add.413, bf16[12,33]{1,0:T(8,128)(2,1)S(1)} %get-tuple-element.269), channel_id=1, replica_groups=mesh['rep'=4,'seq'=4,'grp'=2] {'seq','grp'}, use_global_device_ids=true, to_apply=%region_47.48 | all-reduce | flops 397 | bytes 2384 | tf_op jit(solution)/shard_map/psum | solution.py:1034
  1010.4 3.7 multiply_subtract_fusion.2
  1021.7 3.8 multiply_subtract_fusion.1
  (719 shorter events, 351.0 us)
Async XLA Ops:
  7.2 47.3 %all-gather.6.cloned.1.call-start = ((), (), s32[]{:S(2)}) async-start(), calls=%async_computation.5 | async-start | bytes 3981312 | tf_op jit(solution)/shard_map/all_gather | solution.py:861
  9.3 110.8 %all-gather.8.cloned.1.call-start = ((), (), s32[]{:S(2)}) async-start(), calls=%async_computation.6 | async-start | bytes 1327104 | tf_op jit(solution)/shard_map/all_gather | solution.py:862
  10.1 145.7 %all-reduce.16.cloned.1.call-start = ((), (), s32[]{:S(2)}) async-start(), calls=%async_computation.16 | async-start | bytes 1572864 | tf_op jit(solution)/shard_map/psum | solution.py:832
  98.2 162.3 %all-gather.10.cloned.1.call-start = ((), (), s32[]{:S(2)}) async-start(), calls=%async_computation.7 | async-start | bytes 5308416 | tf_op jit(solution)/shard_map/all_gather | solution.py:863
  99.2 173.2 %all-gather.12.cloned.1.call-start = ((), (), s32[]{:S(2)}) async-start(), calls=%async_computation.8 | async-start | bytes 5308416 | tf_op jit(solution)/shard_map/all_gather | solution.py:864
  100.5 19.5 %copy-start.65 = (bf16[256,768]{1,0:T(8,128)(2,1)S(1)}, bf16[256,768]{1,0:T(8,128)(2,1)}, u32[]{:S(2)}) copy-start(bf16[256,768]{1,0:T(8,128)(2,1)} %x_ref.1) | copy-start | bytes 1179652
  100.5 19.5 %copy-start.98 = (bf16[256,768]{1,0:T(8,128)(2,1)S(1)}, bf16[256,768]{1,0:T(8,128)(2,1)}, u32[]{:S(2)}) copy-start(bf16[256,768]{1,0:T(8,128)(2,1)} %get-tuple-element.28) | copy-start | bytes 1179652
  100.6 272.3 %all-reduce.14.cloned.1.call-start = ((), (), s32[]{:S(2)}) async-start(), calls=%async_computation.15 | async-start | bytes 6291456 | tf_op jit(solution)/shard_map/psum | solution.py:972
  103.0 181.1 %copy-start.179 = (f32[256]{0:T(256)}, f32[256]{0:T(256)S(1)}, u32[]{:S(2)}) copy-start(f32[256]{0:T(256)S(1)} %get-tuple-element.308) | copy-start | bytes 3076
  103.0 181.1 %copy-start.180 = (f32[256]{0:T(256)}, f32[256]{0:T(256)S(1)}, u32[]{:S(2)}) copy-start(f32[256]{0:T(256)S(1)} %get-tuple-element.311) | copy-start | bytes 3076
  103.0 181.1 %copy-start.181 = (f32[256]{0:T(256)}, f32[256]{0:T(256)S(1)}, u32[]{:S(2)}) copy-start(f32[256]{0:T(256)S(1)} %get-tuple-element.312) | copy-start | bytes 3076
  120.1 40.3 %copy-start.51 = (f32[256,256]{0,1:T(8,128)}, f32[256,256]{0,1:T(8,128)S(1)}, u32[]{:S(2)}) copy-start(f32[256,256]{0,1:T(8,128)S(1)} %get-tuple-element.340) | copy-start | bytes 786436
  122.1 161.6 %copy-start.116 = (f32[256]{0:T(256)}, f32[256]{0:T(256)S(1)}, u32[]{:S(2)}) copy-start(f32[256]{0:T(256)S(1)} %broadcast_multiply_fusion.3) | copy-start | bytes 3076
  122.3 161.3 %copy-start.153 = (f32[256]{0:T(256)}, f32[256]{0:T(256)S(1)}, u32[]{:S(2)}) copy-start(f32[256]{0:T(256)S(1)} %fusion.247) | copy-start | bytes 3076
  123.4 36.9 %copy-start.67 = (bf16[256,768]{0,1:T(8,128)(2,1)}, bf16[256,768]{0,1:T(8,128)(2,1)S(1)}, u32[]{:S(2)}) copy-start(bf16[256,768]{0,1:T(8,128)(2,1)S(1)} %copy.466) | copy-start | bytes 1179652
  123.6 36.7 %copy-start.68 = (bf16[256,768]{0,1:T(8,128)(2,1)}, bf16[256,768]{0,1:T(8,128)(2,1)S(1)}, u32[]{:S(2)}) copy-start(bf16[256,768]{0,1:T(8,128)(2,1)S(1)} %copy.467) | copy-start | bytes 1179652
  156.9 54.7 %copy-start.57 = (bf16[256,768]{0,1:T(8,128)(2,1)}, bf16[256,768]{0,1:T(8,128)(2,1)S(1)}, u32[]{:S(2)}) copy-start(bf16[256,768]{0,1:T(8,128)(2,1)S(1)} %copy.464) | copy-start | bytes 1179652
  297.4 287.3 %all-reduce.12.cloned.1.call-start = ((), (), s32[]{:S(2)}) async-start(), calls=%async_computation.14 | async-start | bytes 3145728 | tf_op jit(solution)/shard_map/psum | solution.py:972
  406.1 227.9 %reduce-scatter.10.cloned.1.call-start = ((), (), s32[]{:S(2)}) async-start(), calls=%async_computation.9 | async-start | bytes 2654208 | tf_op jit(solution)/shard_map/reduce_scatter | solution.py:1014
  406.8 167.8 %collective-permute-start.1 = (bf16[16,768]{1,0:T(8,128)(2,1)}, bf16[16,768]{1,0:T(8,128)(2,1)S(1)}, u32[]{:S(2)}, u32[]{:S(2)}) collective-permute-start(bf16[16,768]{1,0:T(8,128)(2,1)} %get-tuple-element.305), channel_id=1, source_target_pairs={{1,0},{2,1},{3,2},{4,3},{5,4},{6,5},{7,6},{9,8},{10,9},{11,10},{12... | collective-permute-start | bytes 73736 | tf_op jit(solution)/shard_map/ppermute | solution.py:41
  408.1 166.5 %collective-permute-start = (bf16[16,768]{1,0:T(8,128)(2,1)}, bf16[16,768]{1,0:T(8,128)(2,1)}, u32[]{:S(2)}, u32[]{:S(2)}) collective-permute-start(bf16[16,768]{1,0:T(8,128)(2,1)} %get-tuple-element.304), channel_id=1, source_target_pairs={{0,1},{1,2},{2,3},{3,4},{4,5},{5,6},{6,7},{8,9},{9,10},{10,11},{11... | collective-permute-start | bytes 73736 | tf_op jit(solution)/shard_map/ppermute | solution.py:39
  415.1 263.6 %reduce-scatter.16.cloned.1.call-start = ((), (), s32[]{:S(2)}) async-start(), calls=%async_computation.12 | async-start | bytes 7962624
  572.2 12.5 %copy-start.77 = (f32[256,768]{0,1:T(8,128)S(1)}, f32[256,768]{0,1:T(8,128)}, u32[]{:S(2)}) copy-start(f32[256,768]{0,1:T(8,128)} %reshape.520) | copy-start | bytes 2359300
  601.5 177.4 %reduce-scatter.12.cloned.1.call-start = ((), (), s32[]{:S(2)}) async-start(), calls=%async_computation.10 | async-start | bytes 10616832 | tf_op jit(solution)/shard_map/reduce_scatter | solution.py:1015
  608.2 270.9 %reduce-scatter.14.cloned.1.call-start = ((), (), s32[]{:S(2)}) async-start(), calls=%async_computation.11 | async-start | bytes 10616832 | tf_op jit(solution)/shard_map/reduce_scatter | solution.py:1016
  615.1 295.9 %reduce-scatter.18.cloned.1.call-start = ((), (), s32[]{:S(2)}) async-start(), calls=%async_computation.13 | async-start | bytes 442368
  631.8 349.4 %all-reduce.18.cloned.1.call-start = ((), (), s32[]{:S(2)}) async-start(), calls=%async_computation.17 | async-start | bytes 3833856 | tf_op jit(solution)/shard_map/psum | solution.py:1020
  631.9 149.1 %copy-start.112 = (f32[12,64,33]{1,0,2:T(8,128)}, f32[12,64,33]{1,0,2:T(8,128)S(1)}, u32[]{:S(2)}) copy-start(f32[12,64,33]{1,0,2:T(8,128)S(1)} %constant_dynamic-update-slice_fusion.11) | copy-start | bytes 304132
  881.3 41.2 %copy-start.89 = (bf16[256,768]{1,0:T(8,128)(2,1)S(1)}, bf16[256,768]{1,0:T(8,128)(2,1)}, u32[]{:S(2)}) copy-start(bf16[256,768]{1,0:T(8,128)(2,1)} %fusion.186) | copy-start | bytes 1179652
  881.3 41.2 %copy-start.91 = (bf16[256,768]{1,0:T(8,128)(2,1)S(1)}, bf16[256,768]{1,0:T(8,128)(2,1)}, u32[]{:S(2)}) copy-start(bf16[256,768]{1,0:T(8,128)(2,1)} %copy-done.90) | copy-start | bytes 1179652
  881.3 41.2 %copy-start.193 = (f32[256]{0:T(256)S(1)}, f32[256]{0:T(256)}, u32[]{:S(2)}) copy-start(f32[256]{0:T(256)} %copy-done.191) | copy-start | bytes 3076
  981.3 29.1 %copy-start.87 = (bf16[96,2304]{0,1:T(8,128)(2,1)S(1)}, bf16[96,2304]{0,1:T(8,128)(2,1)}, u32[]{:S(2)}) copy-start(bf16[96,2304]{0,1:T(8,128)(2,1)} %get-tuple-element.271) | copy-start | bytes 1327108
  (188 other events, 607.8 us)
Sparse Core Ops, SparseCore 0:
  10.3 44.2 all-gather.5
  56.7 28.9 all-gather.7
  98.3 57.3 all-reduce.15
  157.9 51.2 all-gather.9
  211.4 50.5 all-gather.11
  297.5 75.2 all-reduce.13
  406.2 62.0 all-reduce.11
  470.7 35.6 reduce-scatter.9
  601.6 77.0 reduce-scatter.15
  681.0 97.8 reduce-scatter.11
  781.3 97.8 reduce-scatter.13
  882.0 28.9 reduce-scatter.17
  915.6 65.5 all-reduce.17
